TPU v7x, 32 devices: a whole 2x2x4 slice. The times are simulated.
32 devices in a mesh: dp: 2 (over core), row: 4 (over y, x), col: 4 (over z).
Axes of the slice: x: 2, y: 2, z: 4, core: 2. Of those that a mesh axis runs over, the one named last changes fastest.
Arguments:
- tokens: bfloat16 [1536, 8192], P('dp', 'row'), may hold values from -6 to 6
- out_grad: bfloat16 [1536, 8192], P('dp', 'row'), may hold values from -6 to 6
- gate_weight: bfloat16 [8192, 14336], P('row', 'col'), may hold values from -0.0625 to 0.0625
- up_weight: bfloat16 [8192, 14336], P('row', 'col'), may hold values from -0.0625 to 0.0625
- down_weight: bfloat16 [14336, 8192], P('col', 'row'), may hold values from -0.046875 to 0.046875
- gate_mask: int32 [64, 112], P('row', 'col'), may hold values from 0 to 1, as said below
- up_mask: int32 [64, 112], P('row', 'col'), may hold values from 0 to 1, as said below
- down_mask: int32 [112, 64], P('col', 'row'), may hold values from 0 to 1, as said below
Outputs:
- output: bfloat16 [1536, 8192], P(('dp', 'col'), 'row')
- token_grad: bfloat16 [1536, 8192], P(('dp', 'col'), 'row')
- gate_grad: bfloat16 [8192, 14336], P('row', 'col')
- up_grad: bfloat16 [8192, 14336], P('row', 'col')
- down_grad: bfloat16 [14336, 8192], P('col', 'row')
Inputs may be any that keep to these rules, and one draw needn't show every extreme that they name: `gate_mask`: one keep flag for each 128 x 128 block of the matrix; the share kept differs from block row to block row. `up_mask`: one keep flag for each 128 x 128 block of the matrix; the share kept differs from block row to block row. `down_mask`: one keep flag for each 128 x 128 block of the matrix; the share kept differs from block column to block column.
All inputs are finite; a program needn't handle non-finite values.
Results may differ from a plain program's by a relative error of at most 0.029.
Values may be sent and summed in bfloat16 or wider, within the bound.
No kernel may reach another device: no remote copies, remote signals or barrier semaphores. Data moves between devices by JAX's collectives and lax.ppermute only.
A program may use at most 256 MiB of HBM per device.

v0:
```python
import jax
import jax.numpy as jnp
from jax import lax
from jax.sharding import PartitionSpec as P

BLOCK = 128


def expand(mask_tile):
    return jnp.repeat(jnp.repeat(mask_tile, BLOCK, axis=0), BLOCK, axis=1)


def contract_rows(left_side, right_side):
    return lax.dot_general(
        left_side, right_side, (((0,), (0,)), ((), ())), preferred_element_type=jnp.float32
    )


def contract_cols(left_side, right_side):
    return lax.dot_general(
        left_side, right_side, (((1,), (1,)), ((), ())), preferred_element_type=jnp.float32
    )


def body(tokens, out_grad, gate_weight, up_weight, down_weight, gate_mask, up_mask, down_mask):
    gate_keep = expand(gate_mask)
    up_keep = expand(up_mask)
    down_keep = expand(down_mask)
    gate_eff = gate_weight * gate_keep.astype(jnp.bfloat16)
    up_eff = up_weight * up_keep.astype(jnp.bfloat16)
    down_eff = down_weight * down_keep.astype(jnp.bfloat16)
    gate_part = jnp.dot(tokens, gate_eff, preferred_element_type=jnp.float32)
    up_part = jnp.dot(tokens, up_eff, preferred_element_type=jnp.float32)
    gate_share, up_share = (
        lax.psum_scatter(
            gate_part.astype(jnp.bfloat16), "row", scatter_dimension=0, tiled=True
        ).astype(jnp.float32),
        lax.psum_scatter(
            up_part.astype(jnp.bfloat16), "row", scatter_dimension=0, tiled=True
        ).astype(jnp.float32),
    )
    gate_sig = jax.nn.sigmoid(gate_share)
    silu_gate = gate_share * gate_sig
    hidden_share = (silu_gate * up_share).astype(jnp.bfloat16)
    hidden = lax.all_gather(hidden_share, "row", axis=0, tiled=True)
    output = lax.psum_scatter(
        jnp.dot(hidden, down_eff, preferred_element_type=jnp.float32).astype(jnp.bfloat16),
        "col",
        scatter_dimension=0,
        tiled=True,
    )
    down_local = contract_rows(hidden, out_grad) * down_keep.astype(jnp.float32)
    back_part = contract_cols(out_grad, down_eff)
    back_share = lax.psum_scatter(
        back_part.astype(jnp.bfloat16), "row", scatter_dimension=0, tiled=True
    ).astype(jnp.float32)
    gate_deriv = (back_share * up_share * gate_sig * (1.0 + gate_share * (1.0 - gate_sig))).astype(
        jnp.bfloat16
    )
    up_deriv = (back_share * silu_gate).astype(jnp.bfloat16)
    gate_full, up_full = (
        lax.all_gather(gate_deriv, "row", axis=0, tiled=True),
        lax.all_gather(up_deriv, "row", axis=0, tiled=True),
    )
    token_grad = lax.psum_scatter(
        (contract_cols(gate_full, gate_eff) + contract_cols(up_full, up_eff)).astype(jnp.bfloat16),
        "col",
        scatter_dimension=0,
        tiled=True,
    )
    gate_local = contract_rows(tokens, gate_full) * gate_keep.astype(jnp.float32)
    up_local = contract_rows(tokens, up_full) * up_keep.astype(jnp.float32)
    gate_total, up_total, down_total = (
        lax.psum(gate_local.astype(jnp.bfloat16), "dp").astype(jnp.float32),
        lax.psum(up_local.astype(jnp.bfloat16), "dp").astype(jnp.float32),
        lax.psum(down_local.astype(jnp.bfloat16), "dp").astype(jnp.float32),
    )
    return (
        output,
        token_grad,
        gate_total.astype(jnp.bfloat16),
        up_total.astype(jnp.bfloat16),
        down_total.astype(jnp.bfloat16),
    )


def solution(mesh):
    placed = (
        P("dp", "row"),
        P("dp", "row"),
        P("row", "col"),
        P("row", "col"),
        P("col", "row"),
        P("row", "col"),
        P("row", "col"),
        P("col", "row"),
    )
    return jax.shard_map(
        body,
        mesh=mesh,
        in_specs=placed,
        out_specs=(
            P(("dp", "col"), "row"),
            P(("dp", "col"), "row"),
            P("row", "col"),
            P("row", "col"),
            P("col", "row"),
        ),
        check_vma=False,
    )
```

profile of v0, /device:TPU:0, one launch (start us, length us, event | category | flops | bytes accessed | tf_op | source)
XLA Modules:
  0.0 763.5 jit_solution(3192786876345052141)
XLA Ops:
  7.2 0.9 fusion.17
  8.2 0.1 broadcast_in_dim.34
  8.3 9.8 %broadcast_in_dim.35 = bf16[3584,16,128]{2,1,0:T(8,128)(2,1)} broadcast(bf16[3584,16]{1,0:T(8,128)(2,1)S(1)} %bitcast.83), dimensions={0,1} | broadcast | bytes 14794752 | tf_op jit(solution)/shard_map/broadcast_in_dim | solution.py:10
  18.2 21.5 %fusion.5 = bf16[768,3584]{0,1:T(8,128)(2,1)} fusion(bf16[768,2048]{1,0:T(8,128)(2,1)} %param.9, bf16[3584,2048]{1,0:T(8,128)(2,1)} %param.12, bf16[448,8,16,128]{3,2,1,0:T(8,128)(2,1)} %bitcast.80), kind=kOutput, calls=%fused_computation.15 | convolution fusion | flops 11284381696 | bytes 38010880 | tf_op jit(solution)/shard_map/dot_general | solution.py:20
  39.7 8.1 %copy.59 = bf16[768,3584]{1,0:T(8,128)(2,1)} copy(bf16[768,3584]{0,1:T(8,128)(2,1)} %fusion.5) | data formatting | bytes 11010048
  47.9 0.2 reduce-scatter.16.cloned.1.call-start
  48.1 0.4 copy-done.4
  48.6 0.1 broadcast_bitcast_fusion.3
  48.8 19.5 %copy.43 = bf16[2048,3584]{0,1:T(8,128)(2,1)} copy(bf16[2048,3584]{1,0:T(8,128)(2,1)} %param.10) | data formatting | bytes 29360128 | tf_op args[2]
  68.4 7.5 bitcast_multiply_fusion.5
  75.9 5.5 copy-done.2
  81.4 14.0 %fusion.3 = bf16[768,3584]{0,1:T(8,128)(2,1)} fusion(bf16[2048,3584]{0,1:T(8,128)(2,1)S(1)} %bitcast_multiply_fusion.5, bf16[768,2048]{1,0:T(8,128)(2,1)S(1)} %copy-done), kind=kOutput, calls=%fused_computation.13 | convolution fusion | flops 11277041664 | bytes 23330816 | tf_op jit(solution)/shard_map/dot_general | solution.py:32
  95.4 7.9 %copy.55 = bf16[768,3584]{1,0:T(8,128)(2,1)} copy(bf16[768,3584]{0,1:T(8,128)(2,1)} %fusion.3) | data formatting | bytes 11010048
  103.4 0.6 copy-done.5
  104.1 0.1 broadcast_bitcast_fusion.2
  104.3 20.3 %copy.46 = bf16[2048,3584]{0,1:T(8,128)(2,1)} copy(bf16[2048,3584]{1,0:T(8,128)(2,1)} %param.11) | data formatting | bytes 29360128 | tf_op args[3]
  124.6 7.5 bitcast_multiply_fusion.4
  132.1 5.5 copy-done.3
  137.5 14.2 %fusion.4 = bf16[768,3584]{0,1:T(8,128)(2,1)} fusion(bf16[2048,3584]{0,1:T(8,128)(2,1)S(1)} %bitcast_multiply_fusion.4, bf16[768,2048]{1,0:T(8,128)(2,1)S(1)} %copy-done), kind=kOutput, calls=%fused_computation.14 | convolution fusion | flops 11277041664 | bytes 23330816 | tf_op jit(solution)/shard_map/dot_general | solution.py:33
  151.7 8.2 %copy.57 = bf16[768,3584]{1,0:T(8,128)(2,1)} copy(bf16[768,3584]{0,1:T(8,128)(2,1)} %fusion.4) | data formatting | bytes 11010048
  159.9 21.1 %reduce-scatter.16.cloned.1.call-done = bf16[192,3584]{1,0:T(8,128)(2,1)} async-done(((bf16[768,3584]{1,0:T(8,128)(2,1)}), bf16[192,3584]{1,0:T(8,128)(2,1)}) %reduce-scatter.16.cloned.1.call-update) | async-done | bytes 1376272 | tf_op jit(solution)/shard_map/reduce_scatter | solution.py:35
  181.0 66.7 %reduce-scatter.18.cloned.1.call-done = bf16[192,3584]{1,0:T(8,128)(2,1)} async-done(((bf16[768,3584]{1,0:T(8,128)(2,1)}), bf16[192,3584]{1,0:T(8,128)(2,1)}) %reduce-scatter.18.cloned.1.call-update) | async-done | bytes 1376272 | tf_op jit(solution)/shard_map/reduce_scatter | solution.py:38
  247.7 5.7 fusion.12
  253.5 0.5 all-gather.6.cloned.1.call-update
  254.0 0.5 all-gather.4.cloned.1.call-update
  254.6 0.3 all-reduce.3.cloned.1.call-start
  255.1 0.1 broadcast_bitcast_fusion
  255.3 0.1 broadcast_bitcast_fusion.1
  255.5 0.8 copy.64
  256.3 60.9 %all-gather.8.cloned.1.call-done = bf16[768,3584]{1,0:T(8,128)(2,1)} async-done(((bf16[192,3584]{1,0:T(8,128)(2,1)}), bf16[768,3584]{1,0:T(8,128)(2,1)}) %all-gather.8.cloned.1.call-update) | async-done | bytes 5505040 | tf_op jit(solution)/shard_map/all_gather | solution.py:63
  317.2 16.8 %fusion.1 = bf16[2048,3584]{0,1:T(8,128)(2,1)} fusion(bf16[768,3584]{1,0:T(8,128)(2,1)} %all-gather.8.cloned.1.call-done, bf16[768,2048]{1,0:T(8,128)(2,1)S(1)} %copy-done, f32[2048,28]{0,1:T(8,128)S(1)} %bitcast.90), kind=kOutput, calls=%fused_computation.3 | convolution fusion | flops 11288969216 | bytes 23560192 | tf_op jit(solution)/shard_map/dot_general | solution.py:14
  333.9 48.6 %all-gather.6.cloned.1.call-done = bf16[768,3584]{1,0:T(8,128)(2,1)} async-done(((bf16[192,3584]{1,0:T(8,128)(2,1)}), bf16[768,3584]{1,0:T(8,128)(2,1)}) %all-gather.6.cloned.1.call-update) | async-done | bytes 5505040 | tf_op jit(solution)/shard_map/all_gather | solution.py:62
  382.5 16.8 %fusion.2 = bf16[2048,3584]{0,1:T(8,128)(2,1)} fusion(bf16[768,3584]{1,0:T(8,128)(2,1)} %all-gather.6.cloned.1.call-done, bf16[768,2048]{1,0:T(8,128)(2,1)S(1)} %copy-done, f32[2048,28]{0,1:T(8,128)} %bitcast.91), kind=kOutput, calls=%fused_computation.5 | convolution fusion | flops 11288969216 | bytes 23560192 | tf_op jit(solution)/shard_map/dot_general | solution.py:14
  399.3 48.5 %all-gather.4.cloned.1.call-done = bf16[768,3584]{1,0:T(8,128)(2,1)} async-done(((bf16[192,3584]{1,0:T(8,128)(2,1)}), bf16[768,3584]{1,0:T(8,128)(2,1)}) %all-gather.4.cloned.1.call-update) | async-done | bytes 5505040 | tf_op jit(solution)/shard_map/all_gather | solution.py:45
  447.9 0.1 broadcast_in_dim.40
  448.0 11.8 %broadcast_in_dim.41 = f32[3584,16,128]{2,1,0:T(8,128)} broadcast(f32[3584,16]{1,0:T(8,128)S(1)} %bitcast.82), dimensions={0,1} | broadcast | bytes 29589504 | tf_op jit(solution)/shard_map/broadcast_in_dim | solution.py:10
  459.8 24.9 %fusion = bf16[3584,2048]{1,0:T(8,128)(2,1)} fusion(f32[448,8,16,128]{3,2,1,0:T(8,128)} %bitcast.79, bf16[768,3584]{1,0:T(8,128)(2,1)S(1)} %bitcast.93, bf16[768,2048]{1,0:T(8,128)(2,1)S(1)} %copy-done.6), kind=kOutput, calls=%fused_computation.1 | convolution fusion | flops 11288969216 | bytes 52690944 | tf_op jit(solution)/shard_map/dot_general | solution.py:14
  484.7 0.4 reduce-scatter.14.cloned.1.call-start
  485.1 16.4 %fusion.20 = f32[768,2048]{1,0:T(8,128)S(1)} fusion(bf16[768,3584]{1,0:T(8,128)(2,1)} %all-gather.6.cloned.1.call-done, bf16[2048,3584]{0,1:T(8,128)(2,1)} %copy-done.2), kind=kOutput, calls=%fused_computation.40 | convolution fusion | flops 11274289152 | bytes 26476544 | tf_op jit(solution)/shard_map/dot_general | solution.py:20
  501.6 20.5 %add_convert_fusion = bf16[768,2048]{1,0:T(8,128)(2,1)} fusion(f32[768,2048]{1,0:T(8,128)S(1)} %fusion.20, bf16[768,3584]{1,0:T(8,128)(2,1)} %all-gather.8.cloned.1.call-done, bf16[2048,3584]{0,1:T(8,128)(2,1)} %copy-done.3), kind=kOutput, calls=%fused_computation.12 | convolution fusion | flops 11277434880 | bytes 29622272 | tf_op jit(solution)/shard_map/dot_general | solution.py:20
  522.1 0.2 reduce-scatter.12.cloned.1.call-start
  522.3 25.2 %fusion.7 = bf16[768,2048]{1,0:T(8,128)(2,1)} fusion(bf16[768,3584]{1,0:T(8,128)(2,1)} %all-gather.4.cloned.1.call-done, bf16[3584,2048]{1,0:T(8,128)(2,1)} %param.12, bf16[448,8,16,128]{3,2,1,0:T(8,128)(2,1)} %bitcast.81), kind=kOutput, calls=%fused_computation.23 | convolution fusion | flops 11283202048 | bytes 38010880 | tf_op jit(solution)/shard_map/dot_general | solution.py:47
  547.6 67.9 %all-reduce.3.cloned.1.call-done = (bf16[2048,3584]{0,1:T(8,128)(2,1)}, bf16[2048,3584]{0,1:T(8,128)(2,1)}, bf16[3584,2048]{1,0:T(8,128)(2,1)}) async-done(((bf16[2048,3584]{0,1:T(8,128)(2,1)}, bf16[2048,3584]{0,1:T(8,128)(2,1)}, bf16[3584,2048]{1,0:T(8,128)(2,1)}), (bf16[2048,3584]{0,1:T(8,128)(2,1)}, bf16[2048,3584]{0,1:T(8,128)(2,1)}, bf16[3584,2048]{1,0:T(8,128)(2,1)})) %all-reduce.3.cloned.1.call-update) | async-done | bytes 44040208 | tf_op jit(solution)/shard_map/psum | solution.py:74
  615.5 18.9 %copy.53 = bf16[2048,3584]{1,0:T(8,128)(2,1)} copy(bf16[2048,3584]{0,1:T(8,128)(2,1)} %get-tuple-element.25) | data formatting | bytes 29360128
  634.3 18.7 %copy.54 = bf16[2048,3584]{1,0:T(8,128)(2,1)} copy(bf16[2048,3584]{0,1:T(8,128)(2,1)} %get-tuple-element.26) | data formatting | bytes 29360128
  653.0 26.8 %reduce-scatter.14.cloned.1.call-done = bf16[192,2048]{1,0:T(8,128)(2,1)} async-done(((bf16[768,2048]{1,0:T(8,128)(2,1)}), bf16[192,2048]{1,0:T(8,128)(2,1)}) %reduce-scatter.14.cloned.1.call-update) | async-done | bytes 786448 | tf_op jit(solution)/shard_map/reduce_scatter | solution.py:65
  679.8 63.2 %reduce-scatter.12.cloned.1.call-done = bf16[192,2048]{1,0:T(8,128)(2,1)} async-done(((bf16[768,2048]{1,0:T(8,128)(2,1)}), bf16[192,2048]{1,0:T(8,128)(2,1)}) %reduce-scatter.12.cloned.1.call-update) | async-done | bytes 786448 | tf_op jit(solution)/shard_map/reduce_scatter | solution.py:46
  743.0 13.7 %copy.76 = bf16[3584,2048]{1,0:T(8,128)(2,1)} copy(bf16[3584,2048]{1,0:T(8,128)(2,1)} %get-tuple-element.41) | data formatting | bytes 29360128
  (43 shorter events, 1.2 us)
Async XLA Ops:
  7.2 74.2 %copy-start = (bf16[768,2048]{1,0:T(8,128)(2,1)S(1)}, bf16[768,2048]{1,0:T(8,128)(2,1)}, u32[]{:S(2)}) copy-start(bf16[768,2048]{1,0:T(8,128)(2,1)} %param.8) | copy-start | bytes 9437188
  7.2 152.7 %reduce-scatter.20.cloned.1.call-start = ((), (), s32[]{:S(2)}) async-start(), calls=%async_computation.12 | async-start | bytes 6881280 | tf_op jit(solution)/shard_map/reduce_scatter | solution.py:54
  47.8 0.7 copy-start.4
  47.9 133.2 %reduce-scatter.16.cloned.1.call-start = ((), (), s32[]{:S(2)}) async-start(), calls=%async_computation.10 | async-start | bytes 6881280 | tf_op jit(solution)/shard_map/reduce_scatter | solution.py:35
  75.9 5.5 copy-start.2
  103.3 0.7 copy-start.5
  103.3 144.4 %reduce-scatter.18.cloned.1.call-start = ((), (), s32[]{:S(2)}) async-start(), calls=%async_computation.11 | async-start | bytes 6881280 | tf_op jit(solution)/shard_map/reduce_scatter | solution.py:38
  132.0 5.5 copy-start.3
  159.9 157.3 %all-gather.8.cloned.1.call-start = ((), (), s32[]{:S(2)}) async-start(), calls=%async_computation.8 | async-start | bytes 6881280 | tf_op jit(solution)/shard_map/all_gather | solution.py:63
  253.4 129.1 %all-gather.6.cloned.1.call-start = ((), (), s32[]{:S(2)}) async-start(), calls=%async_computation.7 | async-start | bytes 6881280 | tf_op jit(solution)/shard_map/all_gather | solution.py:62
  254.0 193.9 %all-gather.4.cloned.1.call-start = ((), (), s32[]{:S(2)}) async-start(), calls=%async_computation.5 | async-start | bytes 6881280 | tf_op jit(solution)/shard_map/all_gather | solution.py:45
  254.6 360.9 %all-reduce.3.cloned.1.call-start = ((), (), s32[]{:S(2)}) async-start(), calls=%async_computation.13 | async-start | bytes 88080384 | tf_op jit(solution)/shard_map/psum | solution.py:74
  447.9 11.9 %slice-start = ((s8[5505024]{0:T(1024)(128)(4,1)}), s8[4194304]{0:T(1024)(128)(4,1)S(1)}, s32[]{:S(2)}) async-start(s8[5505024]{0:T(1024)(128)(4,1)} %bitcast.92), calls=%async_computation.14 | async-start | bytes 8388608
  448.0 11.8 %slice-start.1 = ((s8[5505024]{0:T(1024)(128)(4,1)}), s8[1310720]{0:T(1024)(128)(4,1)S(1)}, s32[]{:S(2)}) async-start(s8[5505024]{0:T(1024)(128)(4,1)} %bitcast.92), calls=%async_computation.15 | async-start | bytes 2621440
  448.0 11.8 %copy-start.6 = (bf16[768,2048]{1,0:T(8,128)(2,1)S(1)}, bf16[768,2048]{1,0:T(8,128)(2,1)}, u32[]{:S(2)}) copy-start(bf16[768,2048]{1,0:T(8,128)(2,1)} %param.9) | copy-start | bytes 9437188
  484.7 195.1 %reduce-scatter.14.cloned.1.call-start = ((), (), s32[]{:S(2)}) async-start(), calls=%async_computation.9 | async-start | bytes 3932160 | tf_op jit(solution)/shard_map/reduce_scatter | solution.py:65
  522.1 220.9 %reduce-scatter.12.cloned.1.call-start = ((), (), s32[]{:S(2)}) async-start(), calls=%async_computation.6 | async-start | bytes 3932160 | tf_op jit(solution)/shard_map/reduce_scatter | solution.py:46
  743.0 13.8 %copy-start.1 = (bf16[768,2048]{1,0:T(8,128)(2,1)S(1)}, bf16[768,2048]{1,0:T(8,128)(2,1)}, u32[]{:S(2)}) copy-start(bf16[768,2048]{1,0:T(8,128)(2,1)} %param.8) | copy-start | bytes 9437188
Sparse Core Ops, SparseCore 0:
  48.0 66.2 reduce-scatter.19
  117.4 63.6 reduce-scatter.15
  184.1 63.6 reduce-scatter.17
  253.5 63.6 all-gather.7
  318.9 63.6 all-gather.5
  384.2 63.6 all-gather.3
  484.8 130.6 all-reduce.2
  618.3 61.4 reduce-scatter.13
  682.7 60.2 reduce-scatter.11
where the time goes:
time: 772 us; the launch traced here: 763 us
  waiting for transfers between devices  405 us (52%)
  matrix products  170 us (22%)
  local copies, waits for them, and re-layouts  151 us (20%)
  other arithmetic  21.5 us (3%)
  between operations  14.2 us (2%)
    unnamed x38, local copies, waits for them, and re-layouts  129 us
    psum x1, waiting for transfers between devices, body(): lax.psum(gate_local.astype(jnp.bfloat16), 'dp').astype(jnp.float32)  67.9 us
    reduce_scatter x1, waiting for transfers between devices, body(): lax.psum_scatter(up_part.astype(jnp.bfloat16), 'row', scatter_dimension=0...  66.7 us
    reduce_scatter x1, waiting for transfers between devices, body(): lax.psum_scatter(jnp.dot(hidden, down_eff, preferred_element_type=jnp.flo...  63.2 us
    all_gather x1, waiting for transfers between devices, body(): lax.all_gather(up_deriv, 'row', axis=0, tiled=True)  60.9 us
    dot_general x3, matrix products, contract_cols(): lax.dot_general(left_side, right_side, (((1,), (1,)), ((), ())), preferre...  58.5 us
    dot_general x3, matrix products, contract_rows(): lax.dot_general(left_side, right_side, (((0,), (0,)), ((), ())), preferre...  58.4 us
    all_gather x1, waiting for transfers between devices, body(): lax.all_gather(gate_deriv, 'row', axis=0, tiled=True)  48.6 us
  transfers between devices with their start and end apart: 9, of which 8 were waited for; matrix products, arithmetic and copies ran while one was open for 31% of the time, Pallas kernels for 0%

commit v1 on v0

v1 whole, which is shorter than its diff:
```python
import functools

import jax
import jax.numpy as jnp
from jax import lax
from jax.experimental import pallas as pl
from jax.experimental.pallas import tpu as pltpu
from jax.sharding import PartitionSpec as P

BLOCK = 128
TILE = 512
F32 = jnp.float32
BF16 = jnp.bfloat16
ANY = pl.BlockSpec(memory_space=pl.ANY)
SMEM = pl.BlockSpec(memory_space=pltpu.SMEM)


def expand(mask_tile):
    return jnp.repeat(jnp.repeat(mask_tile, BLOCK, axis=0), BLOCK, axis=1)


def dot(left_side, right_side, left_dim=1, right_dim=0):
    return lax.dot_general(
        left_side, right_side, (((left_dim,), (right_dim,)), ((), ())), preferred_element_type=F32
    )


def contract_rows(left_side, right_side):
    return dot(left_side, right_side, 0, 0)


def contract_cols(left_side, right_side):
    return dot(left_side, right_side, 1, 1)


def pair_x(array):
    return lax.ppermute(array, "row", [(i, i ^ 1) for i in range(4)])


def pair_y(array):
    return lax.ppermute(array, "row", [(i, i ^ 2) for i in range(4)])


def pair_z(array, bit):
    return lax.ppermute(array, "col", [(i, i ^ bit) for i in range(4)])


def swap_dp(array):
    return lax.ppermute(array, "dp", [(0, 1), (1, 0)])


def cat(parts, axis=0):
    return lax.concatenate(parts, axis)


def shape_of(*dims):
    return jax.ShapeDtypeStruct(dims, BF16)


def full(array):
    return pl.BlockSpec(array.shape, lambda *at: (0,) * array.ndim)


class Runner:
    def __init__(self):
        self.last = None

    def __call__(self, kernel, grid, args, in_specs, out_shape, out_specs, scratch=(), flops=0, alias=None):
        extra = [] if self.last is None else [self.last]
        count = len(args)

        def wrapped(*refs):
            kernel(*refs[:count], *refs[count + len(extra) :])

        outs = pl.pallas_call(
            wrapped,
            grid=grid,
            in_specs=list(in_specs) + [ANY] * len(extra),
            out_specs=out_specs,
            out_shape=out_shape,
            scratch_shapes=list(scratch),
            input_output_aliases=alias or {},
            compiler_params=pltpu.CompilerParams(vmem_limit_bytes=56 * 1024 * 1024),
            cost_estimate=pl.CostEstimate(flops=flops, bytes_accessed=1 << 20, transcendentals=0),
        )(*args, *extra)
        self.last = outs[0] if isinstance(outs, (tuple, list)) else outs
        return outs


def masked(scr, weight_ref, mask_ref, row_at, col_at):
    rows, cols = weight_ref.shape
    for r in range(rows // BLOCK):
        for c in range(cols // BLOCK):
            at = (slice(r * BLOCK, (r + 1) * BLOCK), slice(c * BLOCK, (c + 1) * BLOCK))
            tile = weight_ref[at]
            scr[at] = jnp.where(mask_ref[row_at + r, col_at + c] > 0, tile, jnp.zeros_like(tile))
    return scr[...]


def store_masked(out_ref, row, grad, mask_ref, row_at, col_at):
    rows, cols = grad.shape
    for r in range(0, rows, BLOCK):
        for c in range(0, cols, BLOCK):
            tile = grad[r : r + BLOCK, c : c + BLOCK]
            kept = mask_ref[row_at + r // BLOCK, col_at + c // BLOCK] > 0
            out_ref[row + r : row + r + BLOCK, c : c + BLOCK] = jnp.where(kept, tile, jnp.zeros_like(tile))


def run_gate_up(run, tokens, gate_weight, up_weight, gate_mask, up_mask, place, lo, hi):
    count, width = tokens.shape
    n, base, share, cols = (hi - lo) // TILE, lo // TILE, count // 4, hi - lo

    def kernel(x_ref, wg_ref, wu_ref, mg_ref, mu_ref, place_ref, s0, s1, s2, g3, u3, w_scr, scr):
        part, j = pl.program_id(0), pl.program_id(1)

        def work(w_ref, m_ref, last):
            weight = masked(w_scr, w_ref, m_ref, 0, (base + j) * (TILE // BLOCK))
            scr[...] = dot(x_ref[...], weight).astype(BF16)
            for k, out in enumerate((s0, s1, s2, last)):
                out[...] = scr[pl.ds(pl.multiple_of((place_ref[0] ^ k) * share, share), share), :]

        pl.when(part == 0)(lambda: work(wg_ref, mg_ref, g3))
        pl.when(part == 1)(lambda: work(wu_ref, mu_ref, u3))

    def first(p, j):
        return (0, jnp.where(p == 0, j, n - 1))

    def second(p, j):
        return (0, jnp.where(p == 0, 0, j))

    both = pl.BlockSpec((share, TILE), lambda p, j: (0, p * n + j))
    return run(
        kernel,
        (2, n),
        (tokens, gate_weight, up_weight, gate_mask, up_mask, place),
        [
            full(tokens),
            pl.BlockSpec((width, TILE), lambda p, j: (0, base + jnp.where(p == 0, j, n - 1))),
            pl.BlockSpec((width, TILE), lambda p, j: (0, base + jnp.where(p == 0, 0, j))),
            SMEM,
            SMEM,
            SMEM,
        ],
        [shape_of(share, 2 * cols)] * 3 + [shape_of(share, cols)] * 2,
        [both] * 3 + [pl.BlockSpec((share, TILE), first), pl.BlockSpec((share, TILE), second)],
        [pltpu.VMEM((width, TILE), BF16), pltpu.VMEM((count, TILE), BF16)],
        flops=4 * count * width * cols,
    )


def run_combine(run, one, two, got_gate, got_up):
    share, cols = got_gate.shape

    def kernel(one_ref, two_ref, gate_ref, up_ref, one_out, two_out):
        one_out[...] = (one_ref[...].astype(F32) + up_ref[...].astype(F32)).astype(BF16)
        two_out[...] = (two_ref[...].astype(F32) + gate_ref[...].astype(F32)).astype(BF16)

    rows = share // 2
    left = pl.BlockSpec((rows, cols), lambda j: (j, 0))
    right = pl.BlockSpec((rows, cols), lambda j: (j, 1))
    return run(
        kernel,
        (2,),
        (one, two, got_gate, got_up),
        [right, left, left, left],
        [shape_of(*one.shape)] * 2,
        [right, left],
        alias={0: 0, 1: 1},
    )


def run_back(run, out_grad, down_weight, down_mask, lo, hi):
    count, width = out_grad.shape
    n, base = (hi - lo) // TILE, lo // TILE

    def kernel(dy_ref, wd_ref, md_ref, out_ref, w_scr):
        j = pl.program_id(0)
        weight = masked(w_scr, wd_ref, md_ref, (base + j) * (TILE // BLOCK), 0)
        out_ref[...] = dot(dy_ref[...], weight, 1, 1).astype(BF16)

    return run(
        kernel,
        (n,),
        (out_grad, down_weight, down_mask),
        [full(out_grad), pl.BlockSpec((TILE, width), lambda j: (base + j, 0)), SMEM],
        shape_of(count, hi - lo),
        pl.BlockSpec((count, TILE), lambda j: (0, j)),
        [pltpu.VMEM((TILE, width), BF16)],
        flops=2 * count * width * (hi - lo),
    )


def add_three(refs, col, width):
    first, second, third = (ref[:, col : col + width].astype(F32) for ref in refs)
    return first + second + third


STEP = 256


def run_hidden(run, sums):
    share = sums[0][0].shape[0]
    widths = [group[0].shape[1] // 2 for group in sums]
    rows = share // 4

    def kernel(*refs):
        out_ref, start = refs[-1], 0
        for i, cols in enumerate(widths):
            group = refs[3 * i : 3 * i + 3]
            for at in range(0, cols, STEP):
                gate, up = add_three(group, at, STEP), add_three(group, cols + at, STEP)
                out_ref[:, start + at : start + at + STEP] = (gate * jax.nn.sigmoid(gate) * up).astype(BF16)
            start += cols

    flat = [array for group in sums for array in group]
    return run(
        kernel,
        (share // rows,),
        flat,
        [pl.BlockSpec((rows, array.shape[1]), lambda j: (j, 0)) for array in flat],
        shape_of(share, sum(widths)),
        pl.BlockSpec((rows, sum(widths)), lambda j: (j, 0)),
    )


def run_derivs(run, sums, back, back_at, row_lo, row_hi):
    cols = sums[0].shape[1] // 2
    rows = 32
    base = row_lo // rows

    def kernel(s0, s1, s2, back_ref, out_ref):
        for at in range(0, cols, STEP):
            gate, up = add_three((s0, s1, s2), at, STEP), add_three((s0, s1, s2), cols + at, STEP)
            grad = back_ref[:, back_at + at : back_at + at + STEP].astype(F32)
            sig = jax.nn.sigmoid(gate)
            silu = gate * sig
            out_ref[:, at : at + STEP] = (grad * up * (sig + silu * (1.0 - sig))).astype(BF16)
            out_ref[:, cols + at : cols + at + STEP] = (grad * silu).astype(BF16)

    return run(
        kernel,
        ((row_hi - row_lo) // rows,),
        (*sums, back),
        [pl.BlockSpec((rows, array.shape[1]), lambda j: (base + j, 0)) for array in (*sums, back)],
        shape_of(row_hi - row_lo, 2 * cols),
        pl.BlockSpec((rows, 2 * cols), lambda j: (j, 0)),
    )


def run_assemble(run, parts, place):
    rows, width = parts[0].shape
    half = rows // 2

    def kernel(*refs):
        place_ref, out_ref = refs[5], refs[6]
        for k, part in enumerate(refs[:5]):
            at = (place_ref[0] ^ min(k, 3)) * rows + (half if k == 4 else 0)
            out_ref[pl.ds(pl.multiple_of(at, half), part.shape[0]), :] = part[...]

    return run(
        kernel,
        (width // TILE,),
        (*parts, place),
        [pl.BlockSpec((part.shape[0], TILE), lambda j: (0, j)) for part in parts] + [SMEM],
        shape_of(4 * rows, width),
        pl.BlockSpec((4 * rows, TILE), lambda j: (0, j)),
    )


def gather_rows(run, own, place):
    half = own.shape[0] // 2
    got_x, got_y = pair_x(own), pair_y(own)
    far = [pair_y(got_x[:half]), pair_x(got_y[half:])]
    return lambda: run_assemble(run, (own, got_x, got_y, *far), place)


def write_col_halves(total, place_ref, keep_ref, send_ref, scr):
    rows = total.shape[0] // 4
    scr[...] = total.astype(BF16)
    low = place_ref[2] & 1
    for i in range(2):
        keep_ref[i * rows : (i + 1) * rows] = scr[pl.ds(pl.multiple_of((2 * i + low) * rows, rows), rows), :]
        send_ref[i * rows : (i + 1) * rows] = scr[pl.ds(pl.multiple_of((2 * i + 1 - low) * rows, rows), rows), :]


def col_halves(count, width):
    spec = pl.BlockSpec((count // 2, TILE), lambda j: (0, j))
    return [shape_of(count // 2, width)] * 2, [spec] * 2, [pltpu.VMEM((count, TILE), BF16)]


def col_scatter(keep, send, col):
    rows = keep.shape[0] // 2
    total = (keep.astype(F32) + pair_z(send, 1).astype(F32)).astype(BF16)
    high = col // 2
    got = pair_z(lax.dynamic_slice_in_dim(total, (1 - high) * rows, rows, 0), 2)
    mine = lax.dynamic_slice_in_dim(total, high * rows, rows, 0)
    return (mine.astype(F32) + got.astype(F32)).astype(BF16)


def run_output(run, hiddens, down_weight, down_mask, place):
    count = hiddens[0].shape[0]
    hidden_units, width = down_weight.shape

    def kernel(*refs):
        h_refs = refs[: len(hiddens)]
        wd_ref, md_ref, place_ref, keep_ref, send_ref, scr, w_scr = refs[len(hiddens) :]
        weight = masked(w_scr, wd_ref, md_ref, 0, pl.program_id(0) * (TILE // BLOCK))
        total, at = None, 0
        for h_ref in h_refs:
            cols = h_ref.shape[1]
            term = dot(h_ref[...], weight[at : at + cols])
            total, at = term if total is None else total + term, at + cols
        write_col_halves(total, place_ref, keep_ref, send_ref, scr)

    shapes, specs, scratch = col_halves(count, width)
    return run(
        kernel,
        (width // TILE,),
        (*hiddens, down_weight, down_mask, place),
        [full(h) for h in hiddens] + [pl.BlockSpec((hidden_units, TILE), lambda j: (0, j)), SMEM, SMEM],
        shapes,
        specs,
        scratch + [pltpu.VMEM((hidden_units, TILE), BF16)],
        flops=2 * count * hidden_units * width,
    )


def run_token_terms(run, derivs, gate_weight, up_weight, gate_mask, up_mask, pieces):
    count = derivs[0].shape[0]
    width = gate_weight.shape[0]
    widths = [d.shape[1] // 2 for d in derivs]
    cols, share = sum(widths), count // 4
    rows = share // pieces

    def kernel(*refs):
        d_refs = refs[: len(derivs)]
        wg_ref, wu_ref, mg_ref, mu_ref = refs[len(derivs) : len(derivs) + 4]
        outs = refs[len(derivs) + 4 : -2]
        row_at = pl.program_id(0) * (TILE // BLOCK)
        gate = masked(refs[-2], wg_ref, mg_ref, row_at, 0)
        up = masked(refs[-1], wu_ref, mu_ref, row_at, 0)
        total, at = None, 0
        for d_ref, here in zip(d_refs, widths):
            term = dot(d_ref[:, :here], gate[:, at : at + here], 1, 1)
            term = term + dot(d_ref[:, here:], up[:, at : at + here], 1, 1)
            total, at = term if total is None else total + term, at + here
        for t, out in enumerate(outs):
            for owner in range(4):
                start = owner * share + t * rows
                out[owner * rows : (owner + 1) * rows] = total[start : start + rows]

    weight_spec = pl.BlockSpec((TILE, cols), lambda j: (j, 0))
    return run(
        kernel,
        (width // TILE,),
        (*derivs, gate_weight, up_weight, gate_mask, up_mask),
        [full(d) for d in derivs] + [weight_spec] * 2 + [SMEM] * 2,
        [jax.ShapeDtypeStruct((4 * rows, width), F32)] * pieces,
        [pl.BlockSpec((4 * rows, TILE), lambda j: (0, j))] * pieces,
        [pltpu.VMEM((TILE, cols), BF16)] * 2,
        flops=4 * count * cols * width,
    )


def run_token_grad(run, deriv, terms, gate_weight, up_weight, gate_mask, up_mask, place, lo):
    count = deriv.shape[0]
    width, cols = gate_weight.shape[0], deriv.shape[1] // 2
    n = cols // TILE

    def kernel(*refs):
        d_ref, terms_ref = refs[:2]
        mg_ref, mu_ref, place_ref, keep_ref, send_ref, scr, w_scr = refs[2 + 2 * n :]
        row_at = pl.program_id(0) * (TILE // BLOCK)
        total = terms_ref[...]
        for i in range(2 * n):
            m_ref = mg_ref if i < n else mu_ref
            weight = masked(w_scr.at[i], refs[2 + i], m_ref, row_at, (lo + (i % n) * TILE) // BLOCK)
            total = total + dot(d_ref[:, i * TILE : (i + 1) * TILE], weight, 1, 1)
        write_col_halves(total, place_ref, keep_ref, send_ref, scr)

    shapes, specs, scratch = col_halves(count, width)
    weight_specs = [pl.BlockSpec((TILE, TILE), functools.partial(lambda q, j: (j, q), lo // TILE + q)) for q in range(n)]
    return run(
        kernel,
        (width // TILE,),
        (deriv, terms, *[gate_weight] * n, *[up_weight] * n, gate_mask, up_mask, place),
        [full(deriv), pl.BlockSpec((count, TILE), lambda j: (0, j))] + weight_specs * 2 + [SMEM] * 3,
        shapes,
        specs,
        scratch + [pltpu.VMEM((2 * n, TILE, TILE), BF16)],
        flops=4 * count * cols * width,
    )


def both_groups(dst, own, other, place_ref, count):
    share = count // 4
    for refs, group in ((own, place_ref[1]), (other, 1 - place_ref[1])):
        if len(refs) == 1:
            dst[pl.ds(pl.multiple_of(group * count, count), count), :] = refs[0][...]
            continue
        rows = share // len(refs)
        for t, ref in enumerate(refs):
            for owner in range(4):
                at = pl.multiple_of(group * count + owner * share + t * rows, rows)
                dst[pl.ds(at, rows), :] = ref[owner * rows : (owner + 1) * rows]


def run_down_grad(run, hid, hid_other, dy_all, down_mask, place, lo, hidden_units, so_far):
    count, cols = hid.shape
    width = dy_all.shape[1]
    n, base = cols // TILE, lo // TILE
    more = [] if so_far is None else [so_far]

    def kernel(*refs):
        h_ref, ho_ref, dy_ref, md_ref, place_ref = refs[:5]
        out_ref, h_all = refs[-2:]
        j = pl.program_id(0)
        both_groups(h_all, (h_ref,), (ho_ref,), place_ref, count)
        left = h_all[...]
        for at in range(0, width, 512):
            grad = dot(left, dy_ref[:, at : at + 512], 0, 0).astype(BF16)
            store_masked(out_ref.at[:, at : at + 512], 0, grad, md_ref, (base + j) * (TILE // BLOCK), at // BLOCK)

    return run(
        kernel,
        (n,),
        (hid, hid_other, dy_all, down_mask, place, *more),
        [pl.BlockSpec((count, TILE), lambda j: (0, j))] * 2 + [full(dy_all), SMEM, SMEM] + [ANY] * len(more),
        shape_of(hidden_units, width),
        pl.BlockSpec((TILE, width), lambda j: (base + j, 0)),
        [pltpu.VMEM((2 * count, TILE), BF16)],
        flops=4 * count * width * cols,
        alias={5: 0} if more else None,
    )


def run_weight_grads(run, xt_all, derivs, others, masks, place, lo, hidden_units, so_far):
    width, all_count = xt_all.shape
    count = all_count // 2
    cols = derivs[0].shape[1] // 2
    n, base, parts = cols // TILE, lo // TILE, len(derivs)
    more = [] if so_far is None else list(so_far)

    def kernel(*refs):
        xt_ref, rest = refs[0], refs[1:]
        own_gate, own_up = rest[:parts], rest[parts : 2 * parts]
        other_gate, other_up = rest[2 * parts : 3 * parts], rest[3 * parts : 4 * parts]
        mg_ref, mu_ref, place_ref = rest[4 * parts : 4 * parts + 3]
        gate_out, up_out, d_all = rest[-3:]
        col_at = (base + pl.program_id(0)) * (TILE // BLOCK)
        for own, other, m_ref, out in (
            (own_gate, other_gate, mg_ref, gate_out),
            (own_up, other_up, mu_ref, up_out),
        ):
            both_groups(d_all, own, other, place_ref, count)
            right = d_all[...]
            for at in range(0, width, 512):
                grad = dot(xt_ref[at : at + 512], right).astype(BF16)
                store_masked(out, at, grad, m_ref, at // BLOCK, col_at)

    gate_specs = [pl.BlockSpec((d.shape[0], TILE), lambda j: (0, j)) for d in derivs]
    up_specs = [pl.BlockSpec((d.shape[0], TILE), lambda j: (0, n + j)) for d in derivs]
    args = (xt_all, *derivs, *derivs, *others, *others, *masks, place, *more)
    return run(
        kernel,
        (n,),
        args,
        [full(xt_all)] + (gate_specs + up_specs) * 2 + [SMEM] * 3 + [ANY] * len(more),
        [shape_of(width, hidden_units)] * 2,
        [pl.BlockSpec((width, TILE), lambda j: (0, base + j))] * 2,
        [pltpu.VMEM((all_count, TILE), BF16)],
        flops=8 * count * width * cols,
        alias={len(args) - 2: 0, len(args) - 1: 1} if more else None,
    )


def fast_body(tokens, out_grad, gate_weight, up_weight, down_weight, gate_mask, up_mask, down_mask):
    run = Runner()
    row, dp, col = (lax.axis_index(name) for name in ("row", "dp", "col"))
    place = jnp.stack([row, dp, col]).astype(jnp.int32)
    count, width = tokens.shape
    share = count // 4
    hidden_units = gate_weight.shape[1]
    masks = (gate_mask, up_mask)
    tiles = hidden_units // TILE
    edges = [0, tiles * 2 // 7 * TILE, tiles * 4 // 7 * TILE, hidden_units]
    pieces = 3
    rows = share // pieces

    def gate_up(i):
        parts = run_gate_up(run, tokens, gate_weight, up_weight, *masks, place, edges[i], edges[i + 1])
        return parts, pair_x(parts[3]), pair_y(parts[4])

    def combine(parts, got_gate, got_up):
        one, two = run_combine(run, parts[1], parts[2], got_gate, got_up)
        return parts[0], pair_x(one), pair_y(two)

    def back(lo, hi):
        part = run_back(run, out_grad, down_weight, down_mask, lo, hi)
        return lax.psum_scatter(part, "row", scatter_dimension=0, tiled=True)

    def hidden(groups):
        return lax.all_gather(run_hidden(run, groups), "row", axis=0, tiled=True)

    def by_group(own):
        other = swap_dp(own)
        return jnp.where(dp == 0, cat([own, other]), cat([other, own]))

    first = gate_up(0)
    back_0 = back(edges[0], edges[1])
    second = gate_up(1)
    sums_0 = combine(*first)
    third = gate_up(2)
    sums_1 = combine(*second)
    hid_0 = hidden([sums_0])
    back_1 = back(edges[1], edges[3])
    sums_2 = combine(*third)
    deriv_0 = gather_rows(run, run_derivs(run, sums_0, back_0, 0, 0, share), place)
    dy_all = by_group(out_grad)
    xt_all = by_group(tokens).T
    hid_0_other = swap_dp(hid_0)
    down_grad = run_down_grad(run, hid_0, hid_0_other, dy_all, down_mask, place, 0, hidden_units, None)
    hid_1 = hidden([sums_1, sums_2])
    deriv_1 = gather_rows(run, run_derivs(run, sums_1, back_1, 0, 0, share), place)
    late = [
        gather_rows(run, run_derivs(run, sums_2, back_1, edges[2] - edges[1], t * rows, (t + 1) * rows), place)
        for t in range(pieces)
    ]
    deriv_0 = deriv_0()
    other_0 = swap_dp(deriv_0)
    grads = run_weight_grads(run, xt_all, [deriv_0], [other_0], masks, place, 0, hidden_units, None)
    hid_1_other = swap_dp(hid_1)
    keep, send = run_output(run, [hid_0, hid_1], down_weight, down_mask, place)
    output = col_scatter(keep, send, col)
    down_grad = run_down_grad(run, hid_1, hid_1_other, dy_all, down_mask, place, edges[1], hidden_units, down_grad)
    deriv_1 = deriv_1()
    other_1 = swap_dp(deriv_1)
    terms = run_token_terms(run, [deriv_0, deriv_1], gate_weight, up_weight, *masks, pieces)
    grads = run_weight_grads(run, xt_all, [deriv_1], [other_1], masks, place, edges[1], hidden_units, grads)
    token_grads, last, last_other = [], [], []
    for t in range(pieces):
        last.append(late[t]())
        last_other.append(swap_dp(last[t]))
        keep, send = run_token_grad(run, last[t], terms[t], gate_weight, up_weight, *masks, place, edges[2])
        token_grads.append(col_scatter(keep, send, col))
    grads = run_weight_grads(run, xt_all, last, last_other, masks, place, edges[2], hidden_units, grads)
    return output, cat(token_grads), *grads, down_grad


def plain_body(
    tokens, out_grad, gate_weight, up_weight, down_weight, gate_mask, up_mask, down_mask
):
    gate_keep = expand(gate_mask)
    up_keep = expand(up_mask)
    down_keep = expand(down_mask)
    gate_eff = gate_weight * gate_keep.astype(BF16)
    up_eff = up_weight * up_keep.astype(BF16)
    down_eff = down_weight * down_keep.astype(BF16)

    def scatter(array, axis):
        return lax.psum_scatter(array.astype(BF16), axis, scatter_dimension=0, tiled=True)

    def gather(array):
        return lax.all_gather(array, "row", axis=0, tiled=True)

    gate_share = scatter(dot(tokens, gate_eff), "row").astype(F32)
    up_share = scatter(dot(tokens, up_eff), "row").astype(F32)
    gate_sig = jax.nn.sigmoid(gate_share)
    silu_gate = gate_share * gate_sig
    hidden = gather((silu_gate * up_share).astype(BF16))
    output = scatter(dot(hidden, down_eff), "col")
    down_local = contract_rows(hidden, out_grad) * down_keep.astype(F32)
    back_share = scatter(contract_cols(out_grad, down_eff), "row").astype(F32)
    gate_deriv = back_share * up_share * gate_sig * (1.0 + gate_share * (1.0 - gate_sig))
    gate_full = gather(gate_deriv.astype(BF16))
    up_full = gather((back_share * silu_gate).astype(BF16))
    token_grad = scatter(contract_cols(gate_full, gate_eff) + contract_cols(up_full, up_eff), "col")
    gate_local = contract_rows(tokens, gate_full) * gate_keep.astype(F32)
    up_local = contract_rows(tokens, up_full) * up_keep.astype(F32)
    totals = [
        lax.psum(local.astype(BF16), "dp") for local in (gate_local, up_local, down_local)
    ]
    return (output, token_grad, *totals)


def solution(mesh):
    wide, tall = P("row", "col"), P("col", "row")
    tok, spread = P("dp", "row"), P(("dp", "col"), "row")
    body = plain_body
    if mesh.shape["row"] == 4 and mesh.shape["dp"] == 2 and mesh.shape["col"] == 4:
        body = fast_body
    return jax.shard_map(
        body,
        mesh=mesh,
        in_specs=(tok, tok, wide, wide, tall, wide, wide, tall),
        out_specs=(spread, spread, wide, wide, tall),
        check_vma=False,
    )
```

time: 772 us -> 604 us (0.78)
  Pallas kernels: 0 us -> 303 us
  waiting for transfers between devices: 405 us -> 172 us
  matrix products: 170 us -> 0 us
  local copies, waits for them, and re-layouts: 151 us -> 37.4 us
  starting transfers between devices: 1.33 us -> 49.8 us
    pallas_call x0 -> x30, Pallas kernels: none -> 303 us  [__call__(): pl.pallas_call(wrapped, grid=grid, in_specs=list(in_specs) + [ANY] * len(...]
    reduce_scatter x5 -> x2, waiting for transfers between devices: 178 us -> 0.68 us  [back(): return lax.psum_scatter(part, 'row', scatter_dimension=0, tiled=True)]
    dot_general x9 -> x0, matrix products: 170 us -> none  [the longest x3 58.5 us: contract_cols(): lax.dot_general(left_side, right_side, (((1,), (1,)), ((), ())), preferre...]
    ppermute x0 -> x49, waiting for transfers between devices: none -> 125 us  [the longest x16 59.2 us: pair_x(): return lax.ppermute(array, 'row', [(i, i ^ 1) for i in range(4)])]
    all_gather x3 -> x2, waiting for transfers between devices: 158 us -> 46 us  [hidden(): return lax.all_gather(run_hidden(run, groups), 'row', axis=0, tiled=True)]
    unnamed x38 -> x81, local copies, waits for them, and re-layouts: 129 us -> 20.1 us
    psum x1 -> x0, waiting for transfers between devices: 67.9 us -> none  [body(): lax.psum(gate_local.astype(jnp.bfloat16), 'dp').astype(jnp.float32)]
    ppermute x0 -> x49, starting transfers between devices: none -> 49.6 us  [the longest x16 18.1 us: pair_x(): return lax.ppermute(array, 'row', [(i, i ^ 1) for i in range(4)])]
  transfers between devices with their start and end apart: 9 -> 53, of which waited for: 8 -> 17; matrix products, arithmetic and copies ran while one was open for 31% -> 8% of each run, Pallas kernels for 0% -> 43%
where the time goes in v1:
time: 604 us; the launch traced here: 600 us
  Pallas kernels  303 us (50%)
  waiting for transfers between devices  172 us (28%)
  starting transfers between devices  49.8 us (8%)
  local copies, waits for them, and re-layouts  37.4 us (6%)
  other arithmetic  23.8 us (4%)
  between operations  14.5 us (2%)
    pallas_call x30, Pallas kernels, __call__(): pl.pallas_call(wrapped, grid=grid, in_specs=list(in_specs) + [ANY] * len(...  303 us
    ppermute x16, waiting for transfers between devices, pair_x(): return lax.ppermute(array, 'row', [(i, i ^ 1) for i in range(4)])  59.2 us
    ppermute x8, waiting for transfers between devices, pair_z(): return lax.ppermute(array, 'col', [(i, i ^ bit) for i in range(4)])  49.7 us
    all_gather x2, waiting for transfers between devices, hidden(): return lax.all_gather(run_hidden(run, groups), 'row', axis=0, tiled=True)  46 us
    unnamed x81, local copies, waits for them, and re-layouts  20.1 us
    ppermute x16, starting transfers between devices, pair_x(): return lax.ppermute(array, 'row', [(i, i ^ 1) for i in range(4)])  18.1 us
    ppermute x16, starting transfers between devices, pair_y(): return lax.ppermute(array, 'row', [(i, i ^ 2) for i in range(4)])  17.7 us
    ppermute x16, waiting for transfers between devices, pair_y(): return lax.ppermute(array, 'row', [(i, i ^ 2) for i in range(4)])  15.7 us
  transfers between devices with their start and end apart: 53, of which 17 were waited for; matrix products, arithmetic and copies ran while one was open for 8% of the time, Pallas kernels for 43%

profile of v1, /device:TPU:0, one launch (start us, length us, event | category | flops | bytes accessed | tf_op | source)
XLA Modules:
  0.0 600.4 jit_solution(10486055309004345327)
XLA Ops:
  7.9 12.7 %shard_map.119 = (bf16[192,2048]{1,0:T(8,128)(2,1)}, bf16[192,2048]{1,0:T(8,128)(2,1)}, bf16[192,2048]{1,0:T(8,128)(2,1)}, bf16[192,1024]{1,0:T(8,128)(2,1)}, bf16[192,1024]{1,0:T(8,128)(2,1)}) custom-call(bf16[768,2048]{1,0:T(8,128)(2,1)} %refs_0_.8, bf16[2048,3584]{1,0:T(8,128)(2,1)} %refs_4_.13, bf16[2048,3584]{1,0:T(8,128)(2,1)} %refs_7_.5, ...), custom_call_target="tpu_custom_call" | custom-call | flops 6442450944 | bytes 1048576 | tf_op jit(solution)/shard_map/pallas_call | solution.py:75
  20.6 3.0 collective-permute-start
  25.7 7.8 %shard_map.120.refs_6_ = bf16[768,1024]{1,0:T(8,128)(2,1)} custom-call(bf16[768,2048]{1,0:T(8,128)(2,1)} %refs_0_.9, bf16[3584,2048]{1,0:T(8,128)(2,1)} %refs_2_.13, s32[28,16]{1,0:T(8,128)} %copy.24.refs_2_.refs_3_, bf16[192,2048]{1,0:T(8,128)(2,1)} %get-tuple-element.43.refs_3_.refs_0_), custom_call_target="tpu_custom_call" | custom-call | flops 3221225472 | bytes 1048576 | tf_op jit(solution)/shard_map/pallas_call | solution.py:75
  33.5 12.8 %shard_map.121 = (bf16[192,2048]{1,0:T(8,128)(2,1)}, bf16[192,2048]{1,0:T(8,128)(2,1)}, bf16[192,2048]{1,0:T(8,128)(2,1)}, bf16[192,1024]{1,0:T(8,128)(2,1)}, bf16[192,1024]{1,0:T(8,128)(2,1)}) custom-call(bf16[768,2048]{1,0:T(8,128)(2,1)} %refs_0_.8, bf16[2048,3584]{1,0:T(8,128)(2,1)} %refs_4_.13, bf16[2048,3584]{1,0:T(8,128)(2,1)} %refs_7_.5, ...), custom_call_target="tpu_custom_call" | custom-call | flops 6442450944 | bytes 1048576 | tf_op jit(solution)/shard_map/pallas_call | solution.py:75
  53.5 28.8 %shard_map.123 = (bf16[192,3072]{1,0:T(8,128)(2,1)}, bf16[192,3072]{1,0:T(8,128)(2,1)}, bf16[192,3072]{1,0:T(8,128)(2,1)}, bf16[192,1536]{1,0:T(8,128)(2,1)}, bf16[192,1536]{1,0:T(8,128)(2,1)}) custom-call(bf16[768,2048]{1,0:T(8,128)(2,1)} %refs_0_.8, bf16[2048,3584]{1,0:T(8,128)(2,1)} %refs_4_.13, bf16[2048,3584]{1,0:T(8,128)(2,1)} %refs_7_.5, ...), custom_call_target="tpu_custom_call" | custom-call | flops 9663676416 | bytes 1048576 | tf_op jit(solution)/shard_map/pallas_call | solution.py:75
  83.2 2.3 shard_map.124
  86.6 3.7 shard_map.125.refs_3_
  91.1 14.1 %shard_map.126.refs_4_ = bf16[768,2560]{1,0:T(8,128)(2,1)} custom-call(bf16[768,2048]{1,0:T(8,128)(2,1)} %refs_0_.9, bf16[3584,2048]{1,0:T(8,128)(2,1)} %refs_2_.13, s32[28,16]{1,0:T(8,128)} %copy.24.refs_2_.refs_3_, bf16[192,1024]{1,0:T(8,128)(2,1)} %shard_map.125.refs_3_), custom_call_target="tpu_custom_call" | custom-call | flops 8053063680 | bytes 1048576 | tf_op jit(solution)/shard_map/pallas_call | solution.py:75
  107.1 2.8 copy.27
  109.9 10.9 %all-gather.3.cloned.1.call-done.refs_0_ = bf16[768,1024]{1,0:T(8,128)(2,1)} async-done(((bf16[192,1024]{1,0:T(8,128)(2,1)}), bf16[768,1024]{1,0:T(8,128)(2,1)}) %all-gather.3.cloned.1.call-update) | async-done | bytes 1572880 | tf_op jit(solution)/shard_map/all_gather | solution.py:503
  124.3 17.7 %collective-permute-done.8.refs_2_ = bf16[192,1536]{1,0:T(8,128)(2,1)S(1)} collective-permute-done((bf16[192,1536]{1,0:T(8,128)(2,1)}, bf16[192,1536]{1,0:T(8,128)(2,1)S(1)}, u32[]{:S(2)}, u32[]{:S(2)}) %collective-permute-start.8) | collective-permute-done | bytes 589856 | tf_op jit(solution)/shard_map/ppermute | solution.py:37
  145.2 2.5 shard_map.127
  149.8 9.5 %maximum_select_fusion = bf16[1536,2048]{0,1:T(8,128)(2,1)} fusion(bf16[768,2048]{0,1:T(8,128)(2,1)} %collective-permute-done.13, bf16[768,2048]{0,1:T(8,128)(2,1)} %copy.27, pred[]{:T(512)S(6)} %eq.4), kind=kLoop, calls=%fused_computation | loop fusion | flops 28311552 | bytes 12582913 | tf_op jit(solution)/shard_map/jit(_where)/select_n | solution.py:507
  159.3 8.7 %copy.29.refs_2_ = bf16[1536,2048]{1,0:T(8,128)(2,1)} copy(bf16[1536,2048]{0,1:T(8,128)(2,1)} %maximum_select_fusion) | data formatting | bytes 12582912 | tf_op jit(solution)/shard_map/jit(_where)/select_n | solution.py:507
  168.0 4.8 shard_map.128.refs_5_.refs_0_
  172.8 11.8 %shard_map.129.refs_6_.refs_5_ = bf16[3584,2048]{1,0:T(8,128)(2,1)} custom-call(bf16[768,1024]{1,0:T(8,128)(2,1)} %all-gather.3.cloned.1.call-done.refs_0_, bf16[768,1024]{1,0:T(8,128)(2,1)} %collective-permute-done.12.refs_1_, bf16[1536,2048]{1,0:T(8,128)(2,1)} %copy.29.refs_2_, s32[28,16]{1,0:T(8,128)} %copy.24.refs_2_.refs_3_, ...), custom_call_target="tpu_custom_call" | custom-call | flops 6442450944 | bytes 1048576 | tf_op jit(solution)/shard_map/pallas_call | solution.py:75
  184.6 19.2 %collective-permute-done.10.refs_4_.refs_1_ = bf16[192,3072]{1,0:T(8,128)(2,1)S(1)} collective-permute-done((bf16[192,3072]{1,0:T(8,128)(2,1)}, bf16[192,3072]{1,0:T(8,128)(2,1)S(1)}, u32[]{:S(2)}, u32[]{:S(2)}) %collective-permute-start.10) | collective-permute-done | bytes 1179680 | tf_op jit(solution)/shard_map/ppermute | solution.py:37
  206.4 5.0 shard_map.130.refs_4_
  213.4 2.8 copy.32
  216.2 22.3 %collective-permute-done.15.refs_1_ = bf16[192,2048]{1,0:T(8,128)(2,1)} collective-permute-done((bf16[192,2048]{1,0:T(8,128)(2,1)}, bf16[192,2048]{1,0:T(8,128)(2,1)}, u32[]{:S(2)}, u32[]{:S(2)}) %collective-permute-start.15) | collective-permute-done | bytes 786464 | tf_op jit(solution)/shard_map/ppermute | solution.py:37
  244.6 5.0 shard_map.131.refs_4_.refs_0_
  251.9 2.5 shard_map.133.refs_4_.refs_0_
  254.3 2.5 shard_map.134.refs_6_.refs_0_
  256.9 4.6 shard_map.135.refs_1_.refs_2_.refs_8_.refs_0_
  261.5 35.1 %all-gather.5.cloned.1.call-done.refs_1_.refs_0_ = bf16[768,2560]{1,0:T(8,128)(2,1)} async-done(((bf16[192,2560]{1,0:T(8,128)(2,1)}), bf16[768,2560]{1,0:T(8,128)(2,1)}) %all-gather.5.cloned.1.call-update) | async-done | bytes 3932176 | tf_op jit(solution)/shard_map/all_gather | solution.py:503
  296.6 7.6 %fusion.refs_0_ = bf16[2048,1536]{1,0:T(8,128)(2,1)} fusion(bf16[768,2048]{0,1:T(8,128)(2,1)} %collective-permute-done.14, bf16[768,2048]{0,1:T(8,128)(2,1)S(1)} %copy-done.3, pred[]{:T(512)S(6)} %eq.4), kind=kLoop, calls=%fused_computation.2 | loop fusion | flops 28311552 | bytes 12582913 | tf_op jit(solution)/shard_map/transpose | solution.py:520
  306.3 19.6 %shard_map.136 = (bf16[2048,3584]{1,0:T(8,128)(2,1)}, bf16[2048,3584]{1,0:T(8,128)(2,1)}) custom-call(bf16[2048,1536]{1,0:T(8,128)(2,1)} %fusion.refs_0_, bf16[768,2048]{1,0:T(8,128)(2,1)} %shard_map.135.refs_1_.refs_2_.refs_8_.refs_0_, bf16[768,2048]{1,0:T(8,128)(2,1)} %shard_map.135.refs_1_.refs_2_.refs_8_.refs_0_, ...), custom_call_target="tpu_custom_call" | custom-call | flops 12884901888 | bytes 1048576 | tf_op jit(solution)/shard_map/pallas_call | solution.py:75
  325.8 19.3 %shard_map.137 = (bf16[384,2048]{1,0:T(8,128)(2,1)}, bf16[384,2048]{1,0:T(8,128)(2,1)}) custom-call(bf16[768,1024]{1,0:T(8,128)(2,1)} %all-gather.3.cloned.1.call-done.refs_0_, bf16[768,2560]{1,0:T(8,128)(2,1)} %all-gather.5.cloned.1.call-done.refs_1_.refs_0_, bf16[3584,2048]{1,0:T(8,128)(2,1)} %refs_2_.13, s32[28,16]{1,0:T(8,128)} %copy.24.refs_2_.refs_3_, ...), custom_call_target="tpu_custom_call" | custom-call | flops 11274289152 | bytes 1048576 | tf_op jit(solution)/shard_map/pallas_call | solution.py:75
  350.9 22.6 %shard_map.138.refs_6_ = bf16[3584,2048]{1,0:T(8,128)(2,1)} custom-call(bf16[768,2560]{1,0:T(8,128)(2,1)} %all-gather.5.cloned.1.call-done.refs_1_.refs_0_, bf16[768,2560]{1,0:T(8,128)(2,1)} %collective-permute-done.30.refs_1_, bf16[1536,2048]{1,0:T(8,128)(2,1)} %copy.29.refs_2_, s32[28,16]{1,0:T(8,128)} %copy.24.refs_2_.refs_3_, ...), custom_call_target="tpu_custom_call", output_to_operand_aliasing={{}: (5, {})} | custom-call | flops 16106127360 | bytes 1048576 | tf_op jit(solution)/shard_map/pallas_call | solution.py:75
  375.8 4.4 shard_map.139.refs_1_.refs_6_.refs_2_
  385.8 2.4 collective-permute-start.21
  394.6 6.0 collective-permute-done.35.refs_2_
  403.7 5.4 collective-permute-done.41.refs_2_
  411.4 11.0 %collective-permute-done.21 = bf16[192,2048]{1,0:T(8,128)(2,1)} collective-permute-done((bf16[192,2048]{1,0:T(8,128)(2,1)}, bf16[192,2048]{1,0:T(8,128)(2,1)}, u32[]{:S(2)}, u32[]{:S(2)}) %collective-permute-start.21) | collective-permute-done | bytes 786464 | tf_op jit(solution)/shard_map/ppermute | solution.py:45
  423.9 2.5 add_convert_fusion.1
  426.4 21.2 %shard_map.140 = (f32[256,2048]{1,0:T(8,128)}, f32[256,2048]{1,0:T(8,128)}, f32[256,2048]{1,0:T(8,128)}) custom-call(bf16[768,2048]{1,0:T(8,128)(2,1)} %shard_map.135.refs_1_.refs_2_.refs_8_.refs_0_, bf16[768,2048]{1,0:T(8,128)(2,1)} %shard_map.139.refs_1_.refs_6_.refs_2_, bf16[2048,3584]{1,0:T(8,128)(2,1)} %refs_4_.13, bf16[2048,3584]{1,0:T(8,128)(2,1)} %refs_7_.5, ...), custom_call_target="tpu_custom_call" | custom-call | flops 12884901888 | bytes 1048576 | tf_op jit(solution)/shard_map/pallas_call | solution.py:75
  449.4 19.7 %shard_map.141 = (bf16[2048,3584]{1,0:T(8,128)(2,1)}, bf16[2048,3584]{1,0:T(8,128)(2,1)}) custom-call(bf16[2048,1536]{1,0:T(8,128)(2,1)} %fusion.refs_0_, bf16[768,2048]{1,0:T(8,128)(2,1)} %shard_map.139.refs_1_.refs_6_.refs_2_, bf16[768,2048]{1,0:T(8,128)(2,1)} %shard_map.139.refs_1_.refs_6_.refs_2_, ...), custom_call_target="tpu_custom_call", output_to_operand_aliasing={{0}: (8, {}), {1}: (9, {})} | custom-call | flops 12884901888 | bytes 1048576 | tf_op jit(solution)/shard_map/pallas_call | solution.py:75
  470.4 4.6 shard_map.142.refs_0_.refs_11_.refs_1_.refs_4_
  475.1 9.9 %shard_map.143 = (bf16[128,2048]{1,0:T(8,128)(2,1)}, bf16[128,2048]{1,0:T(8,128)(2,1)}) custom-call(bf16[256,3072]{1,0:T(8,128)(2,1)} %shard_map.142.refs_0_.refs_11_.refs_1_.refs_4_, f32[256,2048]{1,0:T(8,128)} %get-tuple-element.68.refs_10_.refs_1_, bf16[2048,3584]{1,0:T(8,128)(2,1)} %refs_4_.13, bf16[2048,3584]{1,0:T(8,128)(2,1)} %refs_4_.13, ...), custom_call_target="tpu_custom_call" | custom-call | flops 3221225472 | bytes 1048576 | tf_op jit(solution)/shard_map/pallas_call | solution.py:75
  485.8 4.6 shard_map.144.refs_0_.refs_11_.refs_2_.refs_5_
  491.4 10.0 %shard_map.145 = (bf16[128,2048]{1,0:T(8,128)(2,1)}, bf16[128,2048]{1,0:T(8,128)(2,1)}) custom-call(bf16[256,3072]{1,0:T(8,128)(2,1)} %shard_map.144.refs_0_.refs_11_.refs_2_.refs_5_, f32[256,2048]{1,0:T(8,128)} %get-tuple-element.72.refs_1_, bf16[2048,3584]{1,0:T(8,128)(2,1)} %refs_4_.13, bf16[2048,3584]{1,0:T(8,128)(2,1)} %refs_4_.13, ...), custom_call_target="tpu_custom_call" | custom-call | flops 3221225472 | bytes 1048576 | tf_op jit(solution)/shard_map/pallas_call | solution.py:75
  502.1 4.6 shard_map.146.refs_0_.refs_11_.refs_3_.refs_6_
  508.2 10.1 %shard_map.147 = (bf16[128,2048]{1,0:T(8,128)(2,1)}, bf16[128,2048]{1,0:T(8,128)(2,1)}) custom-call(bf16[256,3072]{1,0:T(8,128)(2,1)} %shard_map.146.refs_0_.refs_11_.refs_3_.refs_6_, f32[256,2048]{1,0:T(8,128)} %get-tuple-element.75.refs_1_, bf16[2048,3584]{1,0:T(8,128)(2,1)} %refs_4_.13, bf16[2048,3584]{1,0:T(8,128)(2,1)} %refs_4_.13, ...), custom_call_target="tpu_custom_call" | custom-call | flops 3221225472 | bytes 1048576 | tf_op jit(solution)/shard_map/pallas_call | solution.py:75
  521.2 3.8 collective-permute-start.33
  525.2 13.1 %collective-permute-done.44 = bf16[128,2048]{1,0:T(8,128)(2,1)S(1)} collective-permute-done((bf16[128,2048]{1,0:T(8,128)(2,1)}, bf16[128,2048]{1,0:T(8,128)(2,1)S(1)}, u32[]{:S(2)}, u32[]{:S(2)}) %collective-permute-start.44) | collective-permute-done | bytes 524320 | tf_op jit(solution)/shard_map/ppermute | solution.py:45
  541.5 17.3 %collective-permute-done.39 = bf16[64,2048]{1,0:T(8,128)(2,1)S(1)} collective-permute-done((bf16[64,2048]{1,0:T(8,128)(2,1)S(1)}, bf16[64,2048]{1,0:T(8,128)(2,1)S(1)}, u32[]{:S(2)}, u32[]{:S(2)}) %collective-permute-start.39) | collective-permute-done | bytes 262176 | tf_op jit(solution)/shard_map/ppermute | solution.py:45
  558.9 4.7 collective-permute-done.45
  566.7 26.9 %shard_map.148 = (bf16[2048,3584]{1,0:T(8,128)(2,1)}, bf16[2048,3584]{1,0:T(8,128)(2,1)}) custom-call(bf16[2048,1536]{1,0:T(8,128)(2,1)} %fusion.refs_0_, bf16[256,3072]{1,0:T(8,128)(2,1)} %shard_map.142.refs_0_.refs_11_.refs_1_.refs_4_, ...), custom_call_target="tpu_custom_call", output_to_operand_aliasing={{0}: (16, {}), {1}: (17, {})} | custom-call | flops 19327352832 | bytes 1048576 | tf_op jit(solution)/shard_map/pallas_call | solution.py:75
  (200 shorter events, 82.1 us)
Async XLA Ops:
  7.2 113.6 %all-gather.3.cloned.1.call-start = ((), (), s32[]{:S(2)}) async-start(), calls=%async_computation.2 | async-start | bytes 1966080 | tf_op jit(solution)/shard_map/all_gather | solution.py:503
  20.6 26.3 %collective-permute-start = (bf16[192,1024]{1,0:T(8,128)(2,1)}, bf16[192,1024]{1,0:T(8,128)(2,1)S(1)}, u32[]{:S(2)}, u32[]{:S(2)}) collective-permute-start(bf16[192,1024]{1,0:T(8,128)(2,1)} %get-tuple-element.46), channel_id=1, source_target_pairs={{0,4},{4,0},{8,12},{12,8},{1,5},{5,1},{9,13},{13,9},{2,6},{6,2},{1... | collective-permute-start | bytes 1179656 | tf_op jit(solution)/shard_map/ppermute | solution.py:37
  23.5 23.4 %collective-permute-start.1 = (bf16[192,1024]{1,0:T(8,128)(2,1)}, bf16[192,1024]{1,0:T(8,128)(2,1)S(1)}, u32[]{:S(2)}, u32[]{:S(2)}) collective-permute-start(bf16[192,1024]{1,0:T(8,128)(2,1)} %get-tuple-element.47), channel_id=1, source_target_pairs={{0,8},{4,12},{8,0},{12,4},{1,9},{5,13},{9,1},{13,5},{2,10},{6,14},... | collective-permute-start | bytes 1179656 | tf_op jit(solution)/shard_map/ppermute | solution.py:41
  46.3 36.0 %collective-permute-start.4 = (bf16[192,1024]{1,0:T(8,128)(2,1)}, bf16[192,1024]{1,0:T(8,128)(2,1)S(1)}, u32[]{:S(2)}, u32[]{:S(2)}) collective-permute-start(bf16[192,1024]{1,0:T(8,128)(2,1)} %get-tuple-element.53), channel_id=1, source_target_pairs={{0,4},{4,0},{8,12},{12,8},{1,5},{5,1},{9,13},{13,9},{2,6},{6,2},{1... | collective-permute-start | bytes 1179656 | tf_op jit(solution)/shard_map/ppermute | solution.py:37
  46.8 35.5 %collective-permute-start.5 = (bf16[192,1024]{1,0:T(8,128)(2,1)}, bf16[192,1024]{1,0:T(8,128)(2,1)S(1)}, u32[]{:S(2)}, u32[]{:S(2)}) collective-permute-start(bf16[192,1024]{1,0:T(8,128)(2,1)} %get-tuple-element.54), channel_id=1, source_target_pairs={{0,8},{4,12},{8,0},{12,4},{1,9},{5,13},{9,1},{13,5},{2,10},{6,14},... | collective-permute-start | bytes 1179656 | tf_op jit(solution)/shard_map/ppermute | solution.py:41
  50.0 35.4 %collective-permute-start.2 = (bf16[192,2048]{1,0:T(8,128)(2,1)}, bf16[192,2048]{1,0:T(8,128)(2,1)S(1)}, u32[]{:S(2)}, u32[]{:S(2)}) collective-permute-start(bf16[192,2048]{1,0:T(8,128)(2,1)} %get-tuple-element.49.refs_6_), channel_id=1, source_target_pairs={{0,4},{4,0},{8,12},{12,8},{1,5},{5,1},{9,13},{13,9},{2,6},{6,2},{1... | collective-permute-start | bytes 2359304 | tf_op jit(solution)/shard_map/ppermute | solution.py:37
  52.0 33.5 %collective-permute-start.3 = (bf16[192,2048]{1,0:T(8,128)(2,1)}, bf16[192,2048]{1,0:T(8,128)(2,1)S(1)}, u32[]{:S(2)}, u32[]{:S(2)}) collective-permute-start(bf16[192,2048]{1,0:T(8,128)(2,1)} %get-tuple-element.50), channel_id=1, source_target_pairs={{0,8},{4,12},{8,0},{12,4},{1,9},{5,13},{9,1},{13,5},{2,10},{6,14},... | collective-permute-start | bytes 2359304 | tf_op jit(solution)/shard_map/ppermute | solution.py:41
  90.3 77.7 %reduce-scatter.3.cloned.1.call-start = ((), (), s32[]{:S(2)}) async-start(), calls=%async_computation.3 | async-start | bytes 1966080 | tf_op jit(solution)/shard_map/reduce_scatter | solution.py:500
  91.1 153.6 %reduce-scatter.5.cloned.1.call-start = ((), (), s32[]{:S(2)}) async-start(), calls=%async_computation.5 | async-start | bytes 4915200 | tf_op jit(solution)/shard_map/reduce_scatter | solution.py:500
  105.3 191.3 %all-gather.5.cloned.1.call-start = ((), (), s32[]{:S(2)}) async-start(), calls=%async_computation.4 | async-start | bytes 4915200 | tf_op jit(solution)/shard_map/all_gather | solution.py:503
  109.9 38.1 %collective-permute-start.13 = (bf16[768,2048]{0,1:T(8,128)(2,1)}, bf16[768,2048]{0,1:T(8,128)(2,1)}, u32[]{:S(2)}, u32[]{:S(2)}) collective-permute-start(bf16[768,2048]{0,1:T(8,128)(2,1)} %copy.27), channel_id=1, source_target_pairs={{0,16},{16,0},{1,17},{17,1},{2,18},{18,2},{3,19},{19,3},{4,20},{20... | collective-permute-start | bytes 9437192 | tf_op jit(solution)/shard_map/ppermute | solution.py:49
  120.8 52.0 %collective-permute-start.12 = (bf16[768,1024]{1,0:T(8,128)(2,1)}, bf16[768,1024]{1,0:T(8,128)(2,1)}, u32[]{:S(2)}, u32[]{:S(2)}) collective-permute-start(bf16[768,1024]{1,0:T(8,128)(2,1)} %all-gather.3.cloned.1.call-done.refs_0_), channel_id=1, source_target_pairs={{0,16},{16,0},{1,17},{17,1},{2,18},{18,2},{3,19},{19,3},{4,20},{20... | collective-permute-start | bytes 4718600 | tf_op jit(solution)/shard_map/ppermute | solution.py:49
  120.8 21.2 %collective-permute-start.8 = (bf16[192,1536]{1,0:T(8,128)(2,1)}, bf16[192,1536]{1,0:T(8,128)(2,1)S(1)}, u32[]{:S(2)}, u32[]{:S(2)}) collective-permute-start(bf16[192,1536]{1,0:T(8,128)(2,1)} %get-tuple-element.60), channel_id=1, source_target_pairs={{0,4},{4,0},{8,12},{12,8},{1,5},{5,1},{9,13},{13,9},{2,6},{6,2},{1... | collective-permute-start | bytes 1769480 | tf_op jit(solution)/shard_map/ppermute | solution.py:37
  122.3 22.0 %collective-permute-start.9 = (bf16[192,1536]{1,0:T(8,128)(2,1)}, bf16[192,1536]{1,0:T(8,128)(2,1)S(1)}, u32[]{:S(2)}, u32[]{:S(2)}) collective-permute-start(bf16[192,1536]{1,0:T(8,128)(2,1)} %get-tuple-element.61), channel_id=1, source_target_pairs={{0,8},{4,12},{8,0},{12,4},{1,9},{5,13},{9,1},{13,5},{2,10},{6,14},... | collective-permute-start | bytes 1769480 | tf_op jit(solution)/shard_map/ppermute | solution.py:41
  122.8 61.8 %collective-permute-start.6 = (bf16[192,2048]{1,0:T(8,128)(2,1)}, bf16[192,2048]{1,0:T(8,128)(2,1)S(1)}, u32[]{:S(2)}, u32[]{:S(2)}) collective-permute-start(bf16[192,2048]{1,0:T(8,128)(2,1)} %get-tuple-element.56.refs_3_), channel_id=1, source_target_pairs={{0,4},{4,0},{8,12},{12,8},{1,5},{5,1},{9,13},{13,9},{2,6},{6,2},{1... | collective-permute-start | bytes 2359304 | tf_op jit(solution)/shard_map/ppermute | solution.py:37
  142.0 42.6 %collective-permute-start.7 = (bf16[192,2048]{1,0:T(8,128)(2,1)}, bf16[192,2048]{1,0:T(8,128)(2,1)S(1)}, u32[]{:S(2)}, u32[]{:S(2)}) collective-permute-start(bf16[192,2048]{1,0:T(8,128)(2,1)} %get-tuple-element.57), channel_id=1, source_target_pairs={{0,8},{4,12},{8,0},{12,4},{1,9},{5,13},{9,1},{13,5},{2,10},{6,14},... | collective-permute-start | bytes 2359304 | tf_op jit(solution)/shard_map/ppermute | solution.py:41
  147.7 56.1 %collective-permute-start.10 = (bf16[192,3072]{1,0:T(8,128)(2,1)}, bf16[192,3072]{1,0:T(8,128)(2,1)S(1)}, u32[]{:S(2)}, u32[]{:S(2)}) collective-permute-start(bf16[192,3072]{1,0:T(8,128)(2,1)} %get-tuple-element.62.refs_4_), channel_id=1, source_target_pairs={{0,4},{4,0},{8,12},{12,8},{1,5},{5,1},{9,13},{13,9},{2,6},{6,2},{1... | collective-permute-start | bytes 3538952 | tf_op jit(solution)/shard_map/ppermute | solution.py:37
  148.0 58.4 %collective-permute-start.11 = (bf16[192,3072]{1,0:T(8,128)(2,1)}, bf16[192,3072]{1,0:T(8,128)(2,1)}, u32[]{:S(2)}, u32[]{:S(2)}) collective-permute-start(bf16[192,3072]{1,0:T(8,128)(2,1)} %get-tuple-element.63), channel_id=1, source_target_pairs={{0,8},{4,12},{8,0},{12,4},{1,9},{5,13},{9,1},{13,5},{2,10},{6,14},... | collective-permute-start | bytes 3538952 | tf_op jit(solution)/shard_map/ppermute | solution.py:41
  211.4 27.1 %collective-permute-start.15 = (bf16[192,2048]{1,0:T(8,128)(2,1)}, bf16[192,2048]{1,0:T(8,128)(2,1)}, u32[]{:S(2)}, u32[]{:S(2)}) collective-permute-start(bf16[192,2048]{1,0:T(8,128)(2,1)} %shard_map.128.refs_5_.refs_0_), channel_id=1, source_target_pairs={{0,4},{4,0},{8,12},{12,8},{1,5},{5,1},{9,13},{13,9},{2,6},{6,2},{1... | collective-permute-start | bytes 2359304 | tf_op jit(solution)/shard_map/ppermute | solution.py:37
  212.3 29.9 %collective-permute-start.16 = (bf16[192,2048]{1,0:T(8,128)(2,1)}, bf16[192,2048]{1,0:T(8,128)(2,1)}, u32[]{:S(2)}, u32[]{:S(2)}) collective-permute-start(bf16[192,2048]{1,0:T(8,128)(2,1)} %shard_map.128.refs_5_.refs_0_), channel_id=1, source_target_pairs={{0,8},{4,12},{8,0},{12,4},{1,9},{5,13},{9,1},{13,5},{2,10},{6,14},... | collective-permute-start | bytes 2359304 | tf_op jit(solution)/shard_map/ppermute | solution.py:41
  216.2 80.4 %collective-permute-start.14 = (bf16[768,2048]{0,1:T(8,128)(2,1)}, bf16[768,2048]{0,1:T(8,128)(2,1)}, u32[]{:S(2)}, u32[]{:S(2)}) collective-permute-start(bf16[768,2048]{0,1:T(8,128)(2,1)} %copy.32), channel_id=1, source_target_pairs={{0,16},{16,0},{1,17},{17,1},{2,18},{18,2},{3,19},{19,3},{4,20},{20... | collective-permute-start | bytes 9437192 | tf_op jit(solution)/shard_map/ppermute | solution.py:49
  239.5 17.4 %collective-permute-start.17 = (bf16[96,2048]{1,0:T(8,128)(2,1)S(1)}, bf16[96,2048]{1,0:T(8,128)(2,1)}, u32[]{:S(2)}, u32[]{:S(2)}) collective-permute-start(bf16[96,2048]{1,0:T(8,128)(2,1)S(1)} %slice.40), channel_id=1, source_target_pairs={{0,8},{4,12},{8,0},{12,4},{1,9},{5,13},{9,1},{13,5},{2,10},{6,14},... | collective-permute-start | bytes 1179656 | tf_op jit(solution)/shard_map/ppermute | solution.py:41
  261.5 44.8 %collective-permute-start.19 = (bf16[768,2048]{1,0:T(8,128)(2,1)}, bf16[768,2048]{1,0:T(8,128)(2,1)}, u32[]{:S(2)}, u32[]{:S(2)}) collective-permute-start(bf16[768,2048]{1,0:T(8,128)(2,1)} %shard_map.135.refs_1_.refs_2_.refs_8_.refs_0_), channel_id=1, source_target_pairs={{0,16},{16,0},{1,17},{17,1},{2,18},{18,2},{3,19},{19,3},{4,20},{20... | collective-permute-start | bytes 9437192 | tf_op jit(solution)/shard_map/ppermute | solution.py:49
  296.6 53.7 %collective-permute-start.30 = (bf16[768,2560]{1,0:T(8,128)(2,1)}, bf16[768,2560]{1,0:T(8,128)(2,1)}, u32[]{:S(2)}, u32[]{:S(2)}) collective-permute-start(bf16[768,2560]{1,0:T(8,128)(2,1)} %all-gather.5.cloned.1.call-done.refs_1_.refs_0_), channel_id=1, source_target_pairs={{0,16},{16,0},{1,17},{17,1},{2,18},{18,2},{3,19},{19,3},{4,20},{20... | collective-permute-start | bytes 11796488 | tf_op jit(solution)/shard_map/ppermute | solution.py:49
  304.2 43.9 %collective-permute-start.26 = (bf16[192,2048]{1,0:T(8,128)(2,1)}, bf16[192,2048]{1,0:T(8,128)(2,1)S(1)}, u32[]{:S(2)}, u32[]{:S(2)}) collective-permute-start(bf16[192,2048]{1,0:T(8,128)(2,1)} %shard_map.131.refs_4_.refs_0_), channel_id=1, source_target_pairs={{0,4},{4,0},{8,12},{12,8},{1,5},{5,1},{9,13},{13,9},{2,6},{6,2},{1... | collective-permute-start | bytes 2359304 | tf_op jit(solution)/shard_map/ppermute | solution.py:37
  305.7 43.0 %collective-permute-start.27 = (bf16[192,2048]{1,0:T(8,128)(2,1)}, bf16[192,2048]{1,0:T(8,128)(2,1)S(1)}, u32[]{:S(2)}, u32[]{:S(2)}) collective-permute-start(bf16[192,2048]{1,0:T(8,128)(2,1)} %shard_map.131.refs_4_.refs_0_), channel_id=1, source_target_pairs={{0,8},{4,12},{8,0},{12,4},{1,9},{5,13},{9,1},{13,5},{2,10},{6,14},... | collective-permute-start | bytes 2359304 | tf_op jit(solution)/shard_map/ppermute | solution.py:41
  345.1 36.6 %collective-permute-start.20 = (bf16[384,2048]{1,0:T(8,128)(2,1)}, bf16[384,2048]{1,0:T(8,128)(2,1)}, u32[]{:S(2)}, u32[]{:S(2)}) collective-permute-start(bf16[384,2048]{1,0:T(8,128)(2,1)} %get-tuple-element.66), channel_id=1, source_target_pairs={{0,1},{1,0},{2,3},{3,2},{4,5},{5,4},{6,7},{7,6},{8,9},{9,8},{10,11... | collective-permute-start | bytes 4718600 | tf_op jit(solution)/shard_map/ppermute | solution.py:45
  346.7 41.6 %collective-permute-start.22 = (bf16[64,3072]{1,0:T(8,128)(2,1)S(1)}, bf16[64,3072]{1,0:T(8,128)(2,1)S(1)}, u32[]{:S(2)}, u32[]{:S(2)}) collective-permute-start(bf16[64,3072]{1,0:T(8,128)(2,1)S(1)} %copy-done.6), channel_id=1, source_target_pairs={{0,4},{4,0},{8,12},{12,8},{1,5},{5,1},{9,13},{13,9},{2,6},{6,2},{1... | collective-permute-start | bytes 1179656 | tf_op jit(solution)/shard_map/ppermute | solution.py:37
  348.1 41.6 %collective-permute-start.23 = (bf16[64,3072]{1,0:T(8,128)(2,1)S(1)}, bf16[64,3072]{1,0:T(8,128)(2,1)S(1)}, u32[]{:S(2)}, u32[]{:S(2)}) collective-permute-start(bf16[64,3072]{1,0:T(8,128)(2,1)S(1)} %copy-done.6), channel_id=1, source_target_pairs={{0,8},{4,12},{8,0},{12,4},{1,9},{5,13},{9,1},{13,5},{2,10},{6,14},... | collective-permute-start | bytes 1179656 | tf_op jit(solution)/shard_map/ppermute | solution.py:41
  348.7 24.8 %collective-permute-start.28 = (bf16[96,2048]{1,0:T(8,128)(2,1)S(1)}, bf16[96,2048]{1,0:T(8,128)(2,1)S(1)}, u32[]{:S(2)}, u32[]{:S(2)}) collective-permute-start(bf16[96,2048]{1,0:T(8,128)(2,1)S(1)} %slice.44), channel_id=1, source_target_pairs={{0,8},{4,12},{8,0},{12,4},{1,9},{5,13},{9,1},{13,5},{2,10},{6,14},... | collective-permute-start | bytes 1179656 | tf_op jit(solution)/shard_map/ppermute | solution.py:41
  350.3 24.8 %collective-permute-start.29 = (bf16[96,2048]{1,0:T(8,128)(2,1)S(1)}, bf16[96,2048]{1,0:T(8,128)(2,1)S(1)}, u32[]{:S(2)}, u32[]{:S(2)}) collective-permute-start(bf16[96,2048]{1,0:T(8,128)(2,1)S(1)} %slice.45), channel_id=1, source_target_pairs={{0,4},{4,0},{8,12},{12,8},{1,5},{5,1},{9,13},{13,9},{2,6},{6,2},{1... | collective-permute-start | bytes 1179656 | tf_op jit(solution)/shard_map/ppermute | solution.py:37
  380.2 67.4 %collective-permute-start.31 = (bf16[768,2048]{1,0:T(8,128)(2,1)}, bf16[768,2048]{1,0:T(8,128)(2,1)S(1)}, u32[]{:S(2)}, u32[]{:S(2)}) collective-permute-start(bf16[768,2048]{1,0:T(8,128)(2,1)} %shard_map.139.refs_1_.refs_6_.refs_2_), channel_id=1, source_target_pairs={{0,16},{16,0},{1,17},{17,1},{2,18},{18,2},{3,19},{19,3},{4,20},{20... | collective-permute-start | bytes 9437192 | tf_op jit(solution)/shard_map/ppermute | solution.py:49
  385.8 36.6 %collective-permute-start.21 = (bf16[192,2048]{1,0:T(8,128)(2,1)}, bf16[192,2048]{1,0:T(8,128)(2,1)}, u32[]{:S(2)}, u32[]{:S(2)}) collective-permute-start(bf16[192,2048]{1,0:T(8,128)(2,1)} %constant_dynamic-slice_fusion.3), channel_id=1, source_target_pairs={{0,2},{1,3},{2,0},{3,1},{4,6},{5,7},{6,4},{7,5},{8,10},{9,11},{10,... | collective-permute-start | bytes 2359304 | tf_op jit(solution)/shard_map/ppermute | solution.py:45
  390.5 18.5 %collective-permute-start.41 = (bf16[64,3072]{1,0:T(8,128)(2,1)}, bf16[64,3072]{1,0:T(8,128)(2,1)}, u32[]{:S(2)}, u32[]{:S(2)}) collective-permute-start(bf16[64,3072]{1,0:T(8,128)(2,1)} %shard_map.134.refs_6_.refs_0_), channel_id=1, source_target_pairs={{0,8},{4,12},{8,0},{12,4},{1,9},{5,13},{9,1},{13,5},{2,10},{6,14},... | collective-permute-start | bytes 1179656 | tf_op jit(solution)/shard_map/ppermute | solution.py:41
  400.6 68.5 %collective-permute-start.24 = (bf16[32,3072]{1,0:T(8,128)(2,1)S(1)}, bf16[32,3072]{1,0:T(8,128)(2,1)S(1)}, u32[]{:S(2)}, u32[]{:S(2)}) collective-permute-start(bf16[32,3072]{1,0:T(8,128)(2,1)S(1)} %slice.42), channel_id=1, source_target_pairs={{0,8},{4,12},{8,0},{12,4},{1,9},{5,13},{9,1},{13,5},{2,10},{6,14},... | collective-permute-start | bytes 589832 | tf_op jit(solution)/shard_map/ppermute | solution.py:41
  403.0 66.7 %collective-permute-start.25 = (bf16[32,3072]{1,0:T(8,128)(2,1)S(1)}, bf16[32,3072]{1,0:T(8,128)(2,1)S(1)}, u32[]{:S(2)}, u32[]{:S(2)}) collective-permute-start(bf16[32,3072]{1,0:T(8,128)(2,1)S(1)} %slice.43), channel_id=1, source_target_pairs={{0,4},{4,0},{8,12},{12,8},{1,5},{5,1},{9,13},{13,9},{2,6},{6,2},{1... | collective-permute-start | bytes 589832 | tf_op jit(solution)/shard_map/ppermute | solution.py:37
  409.0 76.0 %collective-permute-start.36 = (bf16[32,3072]{1,0:T(8,128)(2,1)S(1)}, bf16[32,3072]{1,0:T(8,128)(2,1)S(1)}, u32[]{:S(2)}, u32[]{:S(2)}) collective-permute-start(bf16[32,3072]{1,0:T(8,128)(2,1)S(1)} %slice.46), channel_id=1, source_target_pairs={{0,8},{4,12},{8,0},{12,4},{1,9},{5,13},{9,1},{13,5},{2,10},{6,14},... | collective-permute-start | bytes 589832 | tf_op jit(solution)/shard_map/ppermute | solution.py:41
  422.4 62.6 %collective-permute-start.37 = (bf16[32,3072]{1,0:T(8,128)(2,1)S(1)}, bf16[32,3072]{1,0:T(8,128)(2,1)S(1)}, u32[]{:S(2)}, u32[]{:S(2)}) collective-permute-start(bf16[32,3072]{1,0:T(8,128)(2,1)S(1)} %slice.47), channel_id=1, source_target_pairs={{0,4},{4,0},{8,12},{12,8},{1,5},{5,1},{9,13},{13,9},{2,6},{6,2},{1... | collective-permute-start | bytes 589832 | tf_op jit(solution)/shard_map/ppermute | solution.py:37
  447.6 53.7 %collective-permute-start.42 = (bf16[32,3072]{1,0:T(8,128)(2,1)S(1)}, bf16[32,3072]{1,0:T(8,128)(2,1)S(1)}, u32[]{:S(2)}, u32[]{:S(2)}) collective-permute-start(bf16[32,3072]{1,0:T(8,128)(2,1)S(1)} %slice.48), channel_id=1, source_target_pairs={{0,8},{4,12},{8,0},{12,4},{1,9},{5,13},{9,1},{13,5},{2,10},{6,14},... | collective-permute-start | bytes 589832 | tf_op jit(solution)/shard_map/ppermute | solution.py:41
  469.1 32.3 %collective-permute-start.43 = (bf16[32,3072]{1,0:T(8,128)(2,1)S(1)}, bf16[32,3072]{1,0:T(8,128)(2,1)S(1)}, u32[]{:S(2)}, u32[]{:S(2)}) collective-permute-start(bf16[32,3072]{1,0:T(8,128)(2,1)S(1)} %slice.49), channel_id=1, source_target_pairs={{0,4},{4,0},{8,12},{12,8},{1,5},{5,1},{9,13},{13,9},{2,6},{6,2},{1... | collective-permute-start | bytes 589832 | tf_op jit(solution)/shard_map/ppermute | solution.py:37
  475.1 89.6 %collective-permute-start.46 = (bf16[256,3072]{1,0:T(8,128)(2,1)}, bf16[256,3072]{1,0:T(8,128)(2,1)S(1)}, u32[]{:S(2)}, u32[]{:S(2)}) collective-permute-start(bf16[256,3072]{1,0:T(8,128)(2,1)} %shard_map.142.refs_0_.refs_11_.refs_1_.refs_4_), channel_id=1, source_target_pairs={{0,16},{16,0},{1,17},{17,1},{2,18},{18,2},{3,19},{19,3},{4,20},{20... | collective-permute-start | bytes 4718600 | tf_op jit(solution)/shard_map/ppermute | solution.py:49
  490.4 74.2 %collective-permute-start.47 = (bf16[256,3072]{1,0:T(8,128)(2,1)}, bf16[256,3072]{1,0:T(8,128)(2,1)S(1)}, u32[]{:S(2)}, u32[]{:S(2)}) collective-permute-start(bf16[256,3072]{1,0:T(8,128)(2,1)} %shard_map.144.refs_0_.refs_11_.refs_2_.refs_5_), channel_id=1, source_target_pairs={{0,16},{16,0},{1,17},{17,1},{2,18},{18,2},{3,19},{19,3},{4,20},{20... | collective-permute-start | bytes 4718600 | tf_op jit(solution)/shard_map/ppermute | solution.py:49
  490.9 27.4 %collective-permute-start.32 = (bf16[128,2048]{1,0:T(8,128)(2,1)S(1)}, bf16[128,2048]{1,0:T(8,128)(2,1)S(1)}, u32[]{:S(2)}, u32[]{:S(2)}) collective-permute-start(bf16[128,2048]{1,0:T(8,128)(2,1)S(1)} %copy-done.38), channel_id=1, source_target_pairs={{0,1},{1,0},{2,3},{3,2},{4,5},{5,4},{6,7},{7,6},{8,9},{9,8},{10,11... | collective-permute-start | bytes 1572872 | tf_op jit(solution)/shard_map/ppermute | solution.py:45
  506.7 57.9 %collective-permute-start.48 = (bf16[256,3072]{1,0:T(8,128)(2,1)}, bf16[256,3072]{1,0:T(8,128)(2,1)S(1)}, u32[]{:S(2)}, u32[]{:S(2)}) collective-permute-start(bf16[256,3072]{1,0:T(8,128)(2,1)} %shard_map.146.refs_0_.refs_11_.refs_3_.refs_6_), channel_id=1, source_target_pairs={{0,16},{16,0},{1,17},{17,1},{2,18},{18,2},{3,19},{19,3},{4,20},{20... | collective-permute-start | bytes 4718600 | tf_op jit(solution)/shard_map/ppermute | solution.py:49
  518.3 19.9 %collective-permute-start.44 = (bf16[128,2048]{1,0:T(8,128)(2,1)}, bf16[128,2048]{1,0:T(8,128)(2,1)S(1)}, u32[]{:S(2)}, u32[]{:S(2)}) collective-permute-start(bf16[128,2048]{1,0:T(8,128)(2,1)} %get-tuple-element.77), channel_id=1, source_target_pairs={{0,1},{1,0},{2,3},{3,2},{4,5},{5,4},{6,7},{7,6},{8,9},{9,8},{10,11... | collective-permute-start | bytes 1572872 | tf_op jit(solution)/shard_map/ppermute | solution.py:45
  521.2 18.7 %collective-permute-start.33 = (bf16[64,2048]{1,0:T(8,128)(2,1)S(1)}, bf16[64,2048]{1,0:T(8,128)(2,1)S(1)}, u32[]{:S(2)}, u32[]{:S(2)}) collective-permute-start(bf16[64,2048]{1,0:T(8,128)(2,1)S(1)} %constant_dynamic-slice_fusion.2), channel_id=1, source_target_pairs={{0,2},{1,3},{2,0},{3,1},{4,6},{5,7},{6,4},{7,5},{8,10},{9,11},{10,... | collective-permute-start | bytes 786440 | tf_op jit(solution)/shard_map/ppermute | solution.py:45
  538.2 20.6 %collective-permute-start.39 = (bf16[64,2048]{1,0:T(8,128)(2,1)S(1)}, bf16[64,2048]{1,0:T(8,128)(2,1)S(1)}, u32[]{:S(2)}, u32[]{:S(2)}) collective-permute-start(bf16[64,2048]{1,0:T(8,128)(2,1)S(1)} %constant_dynamic-slice_fusion.1), channel_id=1, source_target_pairs={{0,2},{1,3},{2,0},{3,1},{4,6},{5,7},{6,4},{7,5},{8,10},{9,11},{10,... | collective-permute-start | bytes 786440 | tf_op jit(solution)/shard_map/ppermute | solution.py:45
  539.9 23.7 %collective-permute-start.45 = (bf16[64,2048]{1,0:T(8,128)(2,1)S(1)}, bf16[64,2048]{1,0:T(8,128)(2,1)S(1)}, u32[]{:S(2)}, u32[]{:S(2)}) collective-permute-start(bf16[64,2048]{1,0:T(8,128)(2,1)S(1)} %constant_dynamic-slice_fusion), channel_id=1, source_target_pairs={{0,2},{1,3},{2,0},{3,1},{4,6},{5,7},{6,4},{7,5},{8,10},{9,11},{10,... | collective-permute-start | bytes 786440 | tf_op jit(solution)/shard_map/ppermute | solution.py:45
  (44 other events, 378.9 us)
Sparse Core Ops, SparseCore 0:
  90.4 30.3 all-gather.2
  123.8 43.6 reduce-scatter.2
  171.1 73.4 reduce-scatter.4
  246.3 50.1 all-gather.4
